TPU v7x, 512 devices: a whole 4x8x8 slice. The times are simulated.
512 devices in a mesh: row: 32 (over z, x), src: 16 (over y, core).
Axes of the slice: x: 4, y: 8, z: 8, core: 2. Of those that a mesh axis runs over, the one named last changes fastest.
Arguments:
- shot_fields: bfloat16 [2, 2, 4096, 2048], P(None, None, ('row', 'src')), may hold values from -6 to 6
- diag_inverse: bfloat16 [2, 2, 2048, 2048], P(None, None, 'row', 'src'), may hold values from -0.09375 to 0.09375
- coupling: bfloat16 [2, 2048, 2048], P(None, 'row', 'src'), may hold values from -0.09375 to 0.09375
Outputs:
- solved: bfloat16 [2, 2, 4096, 2048], P(None, None, ('row', 'src'))
All inputs are finite; a program needn't handle non-finite values.
Results may differ from a plain program's by a relative error of at most 0.0049.
Values may be sent and summed in bfloat16 or wider, within the bound.
No kernel may reach another device: no remote copies, remote signals or barrier semaphores. Data moves between devices by JAX's collectives and lax.ppermute only.
A program may use at most 64 MiB of HBM per device.

v0:
```python
import jax
import jax.numpy as jnp
from jax import lax
from jax.sharding import PartitionSpec as P


def complex_product(matrix, vector):
    products = jnp.einsum("csk,drk->cdsr", vector, matrix, preferred_element_type=jnp.float32)
    return jnp.stack([products[0, 0] - products[1, 1], products[1, 0] + products[0, 1]], axis=0)


def fold_with(vector, portion):
    return complex_product(portion, vector)


def on_device(shot_fields, diag_inverse, coupling):
    rows_dev = diag_inverse.shape[2]
    position = lax.axis_index("row")
    gathered = lax.all_gather(shot_fields, "row", axis=2, tiled=True)
    first_in = gathered[:, 0]
    second_in = lax.dynamic_slice_in_dim(gathered[:, 1], position * rows_dev, rows_dev, 2)
    first_sol = fold_with(
        first_in, lax.all_gather(diag_inverse[:, 0], "src", axis=2, tiled=True)
    ).astype(jnp.bfloat16)
    first_all = lax.all_gather(first_sol, "row", axis=2, tiled=True)
    update = fold_with(first_all, lax.all_gather(coupling, "src", axis=2, tiled=True))
    residual = (second_in.astype(jnp.float32) - update).astype(jnp.bfloat16)
    residual_all = lax.all_gather(residual, "row", axis=2, tiled=True)
    second_sol = fold_with(
        residual_all, lax.all_gather(diag_inverse[:, 1], "src", axis=2, tiled=True)
    ).astype(jnp.bfloat16)
    both_sols = jnp.stack([first_sol, second_sol], axis=1)
    return lax.all_to_all(both_sols, "row", split_axis=2, concat_axis=3, tiled=True)


def solution(mesh):
    in_specs = (
        P(None, None, ("row", "src"), None),
        P(None, None, "row", "src"),
        P(None, "row", "src"),
    )
    out_specs = P(None, None, ("row", "src"), None)
    return jax.shard_map(
        on_device, mesh=mesh, in_specs=in_specs, out_specs=out_specs, check_vma=False
    )
```

profile of v0, /device:TPU:8, one launch (start us, length us, event | category | flops | bytes accessed | tf_op | source)
XLA Modules:
  0.0 297.6 jit_solution(9300761867664567833)
XLA Ops:
  6.5 0.0 all-gather.6.cloned.1.call-start
  6.5 1.6 copy.33
  8.1 0.0 all-gather.6.cloned.1.call-update
  8.1 0.0 all-gather.8.cloned.1.call-start
  8.2 0.8 slice_bitcast_fusion.6
  9.0 0.0 copy-start
  9.0 21.4 %all-gather = bf16[2,1,64,2048]{3,2,0,1:T(8,128)(2,1)S(1)} all-gather(bf16[2,1,64,128]{3,2,0,1:T(8,128)(2,1)S(1)} %get-tuple-element.10), channel_id=2, replica_groups=mesh['row'=32,'src'=16] {'src'}, dimensions={3}, use_global_device_ids=true | all-gather | bytes 557056 | tf_op jit(solution)/shard_map/all_gather | solution.py:23
  30.3 73.2 %all-gather.6.cloned.1.call-done = bf16[2,2,256,2048]{3,2,0,1:T(8,128)(2,1)} async-done(((bf16[2,2,8,2048]{3,2,0,1:T(8,128)(2,1)}), bf16[2,2,256,2048]{3,2,0,1:T(8,128)(2,1)}) %all-gather.6.cloned.1.call-update) | async-done | bytes 4194320 | tf_op jit(solution)/shard_map/all_gather | solution.py:19
  103.6 2.4 fusion.11
  106.0 0.6 pad_maximum_fusion
  106.7 0.0 all-gather.8.cloned.1.call-update
  106.7 0.0 all-gather.10.cloned.1.call-start
  106.8 0.0 copy-done
  106.8 17.1 %all_gather.21 = bf16[2,64,2048]{2,1,0:T(8,128)(2,1)S(1)} all-gather(bf16[2,64,128]{2,1,0:T(8,128)(2,1)S(1)} %copy-done), channel_id=1, replica_groups=mesh['row'=32,'src'=16] {'src'}, dimensions={2}, use_global_device_ids=true | all-gather | bytes 557056 | tf_op jit(solution)/shard_map/all_gather | solution.py:26
  123.9 0.0 slice-start
  123.9 63.2 %all-gather.8.cloned.1.call-done = bf16[2,256,2048]{1,2,0:T(8,128)(2,1)} async-done(((bf16[2,256,64]{1,2,0:T(8,128)(2,1)}), bf16[2,256,2048]{1,2,0:T(8,128)(2,1)}) %all-gather.8.cloned.1.call-update) | async-done | bytes 2097168 | tf_op jit(solution)/shard_map/all_gather | solution.py:25
  187.1 2.3 fusion.5
  189.4 0.0 slice-done
  189.4 0.1 fusion.15
  189.6 0.7 copy.38
  190.3 0.0 all-gather.10.cloned.1.call-update
  190.3 17.1 %all-gather.1 = bf16[2,1,64,2048]{3,2,0,1:T(8,128)(2,1)S(1)} all-gather(bf16[2,1,64,128]{3,2,0,1:T(8,128)(2,1)S(1)} %get-tuple-element.9), channel_id=3, replica_groups=mesh['row'=32,'src'=16] {'src'}, dimensions={3}, use_global_device_ids=true | all-gather | bytes 557056 | tf_op jit(solution)/shard_map/all_gather | solution.py:30
  207.5 63.8 %all-gather.10.cloned.1.call-done = bf16[2,256,2048]{1,0,2:T(2,128)(2,1)} async-done(((bf16[2,256,64]{1,0,2:T(2,128)(2,1)}), bf16[2,256,2048]{1,0,2:T(2,128)(2,1)}) %all-gather.10.cloned.1.call-update) | async-done | bytes 2097168 | tf_op jit(solution)/shard_map/all_gather | solution.py:28
  271.3 2.0 fusion.8
  273.4 0.2 copy.41
  273.6 0.2 reshape.146
  273.8 16.0 %all_to_all.18 = bf16[32,2,1024]{2,1,0:T(2,128)(2,1)S(1)} all-to-all(bf16[32,2,1024]{2,1,0:T(2,128)(2,1)S(1)} %reshape.146), channel_id=1, replica_groups=mesh['row'=32,'src'=16] {'row'}, dimensions={0} | all-to-all | bytes 262144 | tf_op jit(solution)/shard_map/all_to_all | solution.py:33
  289.8 0.2 reshape.147
  290.1 0.9 all_to_all.16
  (9 shorter events, 0.2 us)
Async XLA Ops:
  6.5 97.0 %all-gather.6.cloned.1.call-start = ((), (), s32[]{:S(2)}) async-start(), calls=%async_computation.1 | async-start | bytes 4325376 | tf_op jit(solution)/shard_map/all_gather | solution.py:19
  8.1 178.9 %all-gather.8.cloned.1.call-start = ((), (), s32[]{:S(2)}) async-start(), calls=%async_computation.2 | async-start | bytes 2162688 | tf_op jit(solution)/shard_map/all_gather | solution.py:25
  9.0 97.8 %copy-start = (bf16[2,64,128]{2,1,0:T(8,128)(2,1)S(1)}, bf16[2,64,128]{2,1,0:T(8,128)(2,1)}, u32[]{:S(2)}) copy-start(bf16[2,64,128]{2,1,0:T(8,128)(2,1)} %param.5) | copy-start | bytes 98308
  106.7 164.6 %all-gather.10.cloned.1.call-start = ((), (), s32[]{:S(2)}) async-start(), calls=%async_computation.3 | async-start | bytes 2162688 | tf_op jit(solution)/shard_map/all_gather | solution.py:28
  123.9 65.6 %slice-start = ((bf16[2,2,256,2048]{3,2,0,1:T(8,128)(2,1)}), bf16[2,1,256,2048]{3,2,0,1:T(8,128)(2,1)S(1)}, s32[]{:S(2)}) async-start(bf16[2,2,256,2048]{3,2,0,1:T(8,128)(2,1)} %all-gather.6.cloned.1.call-done), calls=%async_computation.4 | async-start | bytes 4194304 | tf_op jit(solution)/shard_map/slice | solution.py:21
Sparse Core Ops, SparseCore 0:
  10.5 92.9 all-gather.5
  106.8 80.2 all-gather.7
  190.5 80.8 all-gather.9
where the time goes:
time: 298 us
  waiting for transfers between devices  200 us (67%)
  blocking collectives  71.6 us (24%)
  between operations  13.2 us (4%)
  matrix products  6.78 us (2%)
  local copies, waits for them, and re-layouts  4.68 us (2%)
    all_gather x1, waiting for transfers between devices, on_device(): gathered = lax.all_gather(shot_fields, 'row', axis=2, tiled=True)  73.2 us
    all_gather x1, waiting for transfers between devices, on_device(): residual_all = lax.all_gather(residual, 'row', axis=2, tiled=True)  63.8 us
    all_gather x1, waiting for transfers between devices, on_device(): first_all = lax.all_gather(first_sol, 'row', axis=2, tiled=True)  63.2 us
    all_gather x1, blocking collectives, on_device(): lax.all_gather(diag_inverse[:, 0], 'src', axis=2, tiled=True)  21.4 us
    all_gather x1, blocking collectives, on_device(): lax.all_gather(diag_inverse[:, 1], 'src', axis=2, tiled=True)  17.1 us
    all_gather x1, blocking collectives, on_device(): lax.all_gather(coupling, 'src', axis=2, tiled=True)  17.1 us
    all_to_all x1, blocking collectives, on_device(): lax.all_to_all(both_sols, 'row', split_axis=2, concat_axis=3, tiled=True)  16 us
    dot_general x3, matrix products, complex_product(): jnp.einsum('csk,drk->cdsr', vector, matrix, preferred_element_type=jnp.fl...  6.78 us
  transfers between devices with their start and end apart: 3, of which 3 were waited for; matrix products, arithmetic and copies ran while one was open for 0% of the time, Pallas kernels for 0%

commit v1 on v0

v1 whole, which is shorter than its diff:
```python
import functools

import jax
import jax.numpy as jnp
from jax import lax
from jax.experimental import pallas as pl
from jax.experimental.pallas import tpu as pltpu
from jax.sharding import Mesh, PartitionSpec as P

F32, BF16 = jnp.float32, jnp.bfloat16
ZH, ZL, X, Y, CORES = 4, 2, 4, 8, 2
GROUP = ZL * X
VMEM_BYTES = 40 * 1024 * 1024
VMEM = pl.BlockSpec(memory_space=pltpu.VMEM)
SMEM = pl.BlockSpec(memory_space=pltpu.SMEM)


def call(body, out_shape, n_in, scalars=0, scratch=(), in_specs=None, flops=0, moved=1 << 20):
    return pl.pallas_call(
        body,
        out_shape=out_shape,
        in_specs=in_specs or [SMEM] * scalars + [VMEM] * (n_in - scalars),
        out_specs=jax.tree.map(lambda _: VMEM, out_shape),
        scratch_shapes=list(scratch),
        compiler_params=pltpu.CompilerParams(vmem_limit_bytes=VMEM_BYTES),
        cost_estimate=pl.CostEstimate(flops=flops, bytes_accessed=moved, transcendentals=0),
    )


def pack_fields(b_ref, out_ref):
    for d in range(GROUP):
        for c in range(2):
            out_ref[d, c, :, 0:2048] = b_ref[c, 0]
            base = d * 64
            for core in range(CORES):
                parts = [
                    b_ref[c, 1, :, zh * 512 + base + core * 32 : zh * 512 + base + core * 32 + 32]
                    for zh in range(ZH)
                ]
                lo = 2048 + core * 128
                out_ref[d, c, :, lo : lo + 128] = jnp.concatenate(parts, axis=-1)


def pack_matrices(diag_ref, coup_ref, out_ref):
    for c in range(2):
        for half in range(CORES):
            rows = slice(half * 32, half * 32 + 32)
            out_ref[half, 0, c] = diag_ref[c, 0, rows]
            out_ref[half, 1, c] = coup_ref[c, rows]
            out_ref[half, 2, c] = diag_ref[c, 1, rows]


def place_matrix(m_ref, mat_ref, which):
    for y in range(Y):
        for core in range(CORES):
            col = (y * 2 + core) * 128
            for c in range(2):
                for zh in range(ZH):
                    row = c * 128 + zh * 32
                    mat_ref[row : row + 32, col : col + 128] = m_ref[y, zh, core, which, c]


def complex_parts(prod):
    real = prod[:128, :128] - prod[128:, 128:]
    imag = prod[:128, 128:] + prod[128:, :128]
    return real, imag


def first_stage(core_ref, own_ref, other_ref, m_ref, rep_ref, first_ref, slice_ref, mat_ref, vec_ref):
    core = core_ref[0]
    place_matrix(m_ref, mat_ref, 0)
    rows_at = pl.multiple_of(2048 + core * 128, 128)
    for ref, who in ((own_ref, core), (other_ref, 1 - core)):
        at = pl.multiple_of(who * 64, 64)
        for c in range(2):
            vec_ref[pl.ds(c * 128 + at, 64), :] = ref[:, c, :, 0:2048].reshape(64, 2048)
            slice_ref[c, pl.ds(at, 64), :] = ref[:, c, :, pl.ds(rows_at, 128)].reshape(64, 128)
    prod = lax.dot_general(
        mat_ref[...], vec_ref[...], (((1,), (1,)), ((), ())), preferred_element_type=F32
    )
    for c, part in enumerate(complex_parts(prod)):
        part = part.astype(BF16)
        for d in range(GROUP):
            rep_ref[d, c] = part
        first_ref[c] = part


def place_fields(core, own_ref, other_ref, vec_ref):
    for ref, who in ((own_ref, core), (other_ref, 1 - core)):
        for d in range(GROUP):
            for zh in range(ZH):
                at = pl.multiple_of(zh * 512 + d * 64 + who * 32, 32)
                for c in range(2):
                    vec_ref[pl.ds(at, 32), c * 128 : c * 128 + 128] = ref[d, c, zh * 32 : zh * 32 + 32]


def second_stage(core_ref, own_ref, other_ref, m_ref, slice_ref, rep_ref, mat_ref, vec_ref):
    place_matrix(m_ref, mat_ref, 0)
    place_fields(core_ref[0], own_ref, other_ref, vec_ref)
    prod = jnp.dot(mat_ref[...], vec_ref[...], preferred_element_type=F32)
    for c, part in enumerate(complex_parts(prod)):
        residual = (slice_ref[c].astype(F32).T - part).astype(BF16)
        for d in range(GROUP):
            rep_ref[d, c] = residual


def third_stage(core_ref, own_ref, other_ref, m_ref, first_ref, out_ref, mat_ref, vec_ref):
    place_matrix(m_ref, mat_ref, 0)
    place_fields(core_ref[0], own_ref, other_ref, vec_ref)
    prod = jnp.dot(mat_ref[...], vec_ref[...], preferred_element_type=F32)
    for c, part in enumerate(complex_parts(prod)):
        for p, value in ((0, first_ref[c].astype(F32)), (1, part)):
            out_ref[:, c, p] = value.T.reshape(CORES * GROUP, 8, 128).astype(BF16)


def unpack(in_ref, out_ref):
    for c in range(2):
        for p in range(2):
            for zh in range(ZH):
                for pair in range(GROUP // 2):
                    parts = [
                        in_ref[core, 2 * pair + d, c, p, :, zh * 32 : zh * 32 + 32]
                        for d in range(2)
                        for core in range(CORES)
                    ]
                    at = zh * 512 + pair * 128
                    out_ref[c, p, :, at : at + 128] = jnp.concatenate(parts, axis=-1)


def gather_group(block):
    own = lax.all_to_all(block, ("zl", "x"), 0, 0, tiled=True)
    return own, lax.ppermute(own, "core", [(0, 1), (1, 0)])


def on_device(shot_fields, diag_inverse, coupling):
    shape = jax.ShapeDtypeStruct
    core = lax.axis_index("core").reshape(1)

    mats = call(pack_matrices, shape((2, 3, 2, 32, 128), BF16), 2)(diag_inverse, coupling)
    mats = lax.all_to_all(mats, "core", 0, 0, tiled=True)
    mats = jnp.broadcast_to(mats[None], (ZH,) + mats.shape)
    mats = lax.all_to_all(mats, "zh", 0, 0, tiled=True)
    mats = lax.all_gather(mats, "y", axis=0)

    fields = call(pack_fields, shape((GROUP, 2, 8, 2304), BF16), 1)(shot_fields)
    own, other = gather_group(fields)

    scratch = [pltpu.VMEM((256, 2048), BF16), pltpu.VMEM((256, 2048), BF16)]
    flops = 2 * 256 * 256 * 2048

    def mat_spec(which):
        return pl.BlockSpec((Y, ZH, CORES, 1, 2, 32, 128), lambda i: (0, 0, 0, which, 0, 0, 0))

    def whole(a):
        return pl.BlockSpec(a, lambda i: (0,) * len(a))

    def stage(body, which, outs, *args):
        specs = [SMEM] + [whole(a.shape) for a in args[:2]] + [mat_spec(which)]
        specs += [whole(a.shape) for a in args[2:]]
        vec = (256, 2048) if which == 0 else (2048, 256)
        return pl.pallas_call(
            body,
            grid=(1,),
            out_shape=outs,
            in_specs=specs,
            out_specs=jax.tree.map(lambda o: whole(o.shape), outs),
            scratch_shapes=[pltpu.VMEM((256, 2048), BF16), pltpu.VMEM(vec, BF16)],
            compiler_params=pltpu.CompilerParams(vmem_limit_bytes=VMEM_BYTES),
            cost_estimate=pl.CostEstimate(flops=flops, bytes_accessed=3 << 20, transcendentals=0),
        )(core, args[0], args[1], mats, *args[2:])

    rep = shape((GROUP, 2, 128, 128), BF16)
    block = shape((2, 128, 128), BF16)
    first_rep, first, second_slice = stage(first_stage, 0, (rep, block, block), own, other)
    own, other = gather_group(first_rep)
    residual_rep = stage(second_stage, 1, rep, own, other, second_slice)
    own, other = gather_group(residual_rep)
    both = stage(third_stage, 2, shape((CORES * GROUP, 2, 2, 8, 128), BF16), own, other, first)

    both = lax.all_to_all(both.reshape(CORES, GROUP, 2, 2, 8, 128), "core", 0, 0, tiled=True)
    both = lax.all_to_all(both, ("zl", "x"), 1, 1, tiled=True)
    return call(unpack, shape((2, 2, 8, 2048), BF16), 1)(both)


def solution(mesh):
    axes = ("zh", "zl", "x", "y", "core")
    fine = Mesh(mesh.devices.reshape(ZH, ZL, X, Y, CORES), axes)
    row, src = ("zh", "zl", "x"), ("y", "core")
    in_specs = (
        P(None, None, row + src, None),
        P(None, None, row, src),
        P(None, row, src),
    )
    out_specs = P(None, None, row + src, None)
    return jax.shard_map(
        on_device, mesh=fine, in_specs=in_specs, out_specs=out_specs, check_vma=False
    )
```

time: 298 us -> 142 us (0.48)
  the two profiles are of different devices: /device:TPU:8 before, /device:TPU:24 now
where the time goes in v1:
time: 142 us; the launch traced here: 141 us
  blocking collectives  84.4 us (59%)
  waiting for transfers between devices  29.9 us (21%)
  between operations  13.5 us (10%)
  starting transfers between devices  5.73 us (4%)
  local copies, waits for them, and re-layouts  4.48 us (3%)
  Pallas kernels  3.4 us (2%)
    all_to_all x3, blocking collectives, gather_group(): own = lax.all_to_all(block, ('zl', 'x'), 0, 0, tiled=True)  42.8 us
    all_to_all x1, blocking collectives, on_device(): mats = lax.all_to_all(mats, 'zh', 0, 0, tiled=True)  24.8 us
    all_gather x1, waiting for transfers between devices, on_device(): mats = lax.all_gather(mats, 'y', axis=0)  24.2 us
    all_to_all x1, blocking collectives, on_device(): both = lax.all_to_all(both, ('zl', 'x'), 1, 1, tiled=True)  9.17 us
    ppermute x3, starting transfers between devices, gather_group(): return (own, lax.ppermute(own, 'core', [(0, 1), (1, 0)]))  5.73 us
    ppermute x3, waiting for transfers between devices, gather_group(): return (own, lax.ppermute(own, 'core', [(0, 1), (1, 0)]))  5.72 us
    unnamed x10, local copies, waits for them, and re-layouts  4.39 us
    all_to_all x1, blocking collectives, on_device(): lax.all_to_all(both.reshape(CORES, GROUP, 2, 2, 8, 128), 'core', 0, 0, ti...  3.84 us
  transfers between devices with their start and end apart: 4, of which 4 were waited for; matrix products, arithmetic and copies ran while one was open for 0% of the time, Pallas kernels for 0%

profile of v1, /device:TPU:24, one launch (start us, length us, event | category | flops | bytes accessed | tf_op | source)
XLA Modules:
  0.0 141.4 jit_solution(12575717104031537016)
XLA Ops:
  6.5 0.0 all-gather.3.cloned.1.call-start
  6.5 0.0 copy-start.3
  6.5 0.8 copy-done.3
  7.4 0.0 copy-start.4
  7.4 0.8 copy-done.4
  8.1 3.8 %all_to_all.35 = bf16[2,3,2,32,128]{4,3,2,1,0:T(8,128)(2,1)S(1)} all-to-all(bf16[2,3,2,32,128]{4,3,2,1,0:T(8,128)(2,1)S(1)} %shard_map.38), channel_id=1, replica_groups=mesh['zh'=4,'zl'=2,'x'=4,'y'=8,'core'=2] {'core'}, dimensions={0} | all-to-all | bytes 196608 | tf_op jit(solution)/shard_map/all_to_all | solution.py:140
  11.9 0.1 broadcast_in_dim.2
  12.0 24.8 %all_to_all.36 = bf16[4,2,3,2,32,128]{5,4,3,2,1,0:T(8,128)(2,1)} all-to-all(bf16[4,2,3,2,32,128]{5,4,3,2,1,0:T(8,128)(2,1)S(1)} %broadcast_in_dim.2), channel_id=1, replica_groups=mesh['zh'=4,'zl'=2,'x'=4,'y'=8,'core'=2] {'zh'}, dimensions={0} | all-to-all | bytes 786432 | tf_op jit(solution)/shard_map/all_to_all | solution.py:142
  36.9 0.0 all-gather.3.cloned.1.call-update
  36.9 0.0 copy-start.2
  36.9 0.9 copy-done.2
  37.8 0.2 shard_map.37
  38.0 14.4 %all_to_all.37.own_ref = bf16[8,2,8,2304]{3,2,1,0:T(8,128)(2,1)S(1)} all-to-all(bf16[8,2,8,2304]{3,2,1,0:T(8,128)(2,1)S(1)} %shard_map.37), channel_id=1, replica_groups=mesh['zh'=4,'zl'=2,'x'=4,'y'=8,'core'=2] {'zl','x'}, dimensions={0} | all-to-all | bytes 1179648 | tf_op jit(solution)/shard_map/all_to_all | solution.py:131
  52.4 1.9 %collective-permute-start = (bf16[8,2,8,2304]{3,2,1,0:T(8,128)(2,1)S(1)}, bf16[8,2,8,2304]{3,2,1,0:T(8,128)(2,1)S(1)}, u32[]{:S(2)}, u32[]{:S(2)}) collective-permute-start(bf16[8,2,8,2304]{3,2,1,0:T(8,128)(2,1)S(1)} %all_to_all.37.own_ref), channel_id=1, source_target_pairs={{0,1},{1,0},{2,3},{3,2},{4,5},{5,4},{6,7},{7,6},{8,9},{9,8},{10,11... | collective-permute-start | bytes 1769480 | tf_op jit(solution)/shard_map/ppermute | solution.py:132
  54.3 2.0 %collective-permute-done.other_ref = bf16[8,2,8,2304]{3,2,1,0:T(8,128)(2,1)S(1)} collective-permute-done((bf16[8,2,8,2304]{3,2,1,0:T(8,128)(2,1)S(1)}, bf16[8,2,8,2304]{3,2,1,0:T(8,128)(2,1)S(1)}, u32[]{:S(2)}, u32[]{:S(2)}) %collective-permute-start) | collective-permute-done | bytes 589856 | tf_op jit(solution)/shard_map/ppermute | solution.py:132
  56.3 24.2 %all-gather.3.cloned.1.call-done = bf16[32,2,3,2,32,128]{5,4,3,2,1,0:T(8,128)(2,1)} async-done(((bf16[4,2,3,2,32,128]{5,4,3,2,1,0:T(8,128)(2,1)}), bf16[32,2,3,2,32,128]{5,4,3,2,1,0:T(8,128)(2,1)}) %all-gather.3.cloned.1.call-update) | async-done | bytes 3145744 | tf_op jit(solution)/shard_map/all_gather | solution.py:143
  80.5 0.0 copy-start
  80.5 1.9 %copy-done = bf16[32,2,3,2,32,128]{5,4,3,2,1,0:T(8,128)(2,1)S(1)} copy-done((bf16[32,2,3,2,32,128]{5,4,3,2,1,0:T(8,128)(2,1)S(1)}, bf16[32,2,3,2,32,128]{5,4,3,2,1,0:T(8,128)(2,1)}, u32[]{:S(2)}) %copy-start) | copy-done | bytes 3145752
  82.4 0.0 copy-start.1
  82.4 0.7 shard_map.39
  83.1 15.3 %all_to_all.38.own_ref = bf16[8,2,128,128]{3,2,1,0:T(8,128)(2,1)S(1)} all-to-all(bf16[8,2,128,128]{3,2,1,0:T(8,128)(2,1)S(1)} %get-tuple-element.8), channel_id=1, replica_groups=mesh['zh'=4,'zl'=2,'x'=4,'y'=8,'core'=2] {'zl','x'}, dimensions={0} | all-to-all | bytes 1048576 | tf_op jit(solution)/shard_map/all_to_all | solution.py:131
  98.4 1.9 %collective-permute-start.1 = (bf16[8,2,128,128]{3,2,1,0:T(8,128)(2,1)S(1)}, bf16[8,2,128,128]{3,2,1,0:T(8,128)(2,1)S(1)}, u32[]{:S(2)}, u32[]{:S(2)}) collective-permute-start(bf16[8,2,128,128]{3,2,1,0:T(8,128)(2,1)S(1)} %all_to_all.38.own_ref), channel_id=1, source_target_pairs={{0,1},{1,0},{2,3},{3,2},{4,5},{5,4},{6,7},{7,6},{8,9},{9,8},{10,11... | collective-permute-start | bytes 1572872 | tf_op jit(solution)/shard_map/ppermute | solution.py:132
  100.3 1.9 %collective-permute-done.1.other_ref = bf16[8,2,128,128]{3,2,1,0:T(8,128)(2,1)S(1)} collective-permute-done((bf16[8,2,128,128]{3,2,1,0:T(8,128)(2,1)S(1)}, bf16[8,2,128,128]{3,2,1,0:T(8,128)(2,1)S(1)}, u32[]{:S(2)}, u32[]{:S(2)}) %collective-permute-start.1) | collective-permute-done | bytes 524320 | tf_op jit(solution)/shard_map/ppermute | solution.py:132
  102.2 0.0 copy-done.1
  102.2 0.8 shard_map.40
  103.0 13.0 %all_to_all.39.own_ref = bf16[8,2,128,128]{3,2,1,0:T(8,128)(2,1)S(1)} all-to-all(bf16[8,2,128,128]{3,2,1,0:T(8,128)(2,1)S(1)} %shard_map.40), channel_id=1, replica_groups=mesh['zh'=4,'zl'=2,'x'=4,'y'=8,'core'=2] {'zl','x'}, dimensions={0} | all-to-all | bytes 1048576 | tf_op jit(solution)/shard_map/all_to_all | solution.py:131
  116.0 1.9 %collective-permute-start.2 = (bf16[8,2,128,128]{3,2,1,0:T(8,128)(2,1)S(1)}, bf16[8,2,128,128]{3,2,1,0:T(8,128)(2,1)S(1)}, u32[]{:S(2)}, u32[]{:S(2)}) collective-permute-start(bf16[8,2,128,128]{3,2,1,0:T(8,128)(2,1)S(1)} %all_to_all.39.own_ref), channel_id=1, source_target_pairs={{0,1},{1,0},{2,3},{3,2},{4,5},{5,4},{6,7},{7,6},{8,9},{9,8},{10,11... | collective-permute-start | bytes 1572872 | tf_op jit(solution)/shard_map/ppermute | solution.py:132
  117.9 1.9 %collective-permute-done.2.other_ref = bf16[8,2,128,128]{3,2,1,0:T(8,128)(2,1)S(1)} collective-permute-done((bf16[8,2,128,128]{3,2,1,0:T(8,128)(2,1)S(1)}, bf16[8,2,128,128]{3,2,1,0:T(8,128)(2,1)S(1)}, u32[]{:S(2)}, u32[]{:S(2)}) %collective-permute-start.2) | collective-permute-done | bytes 524320 | tf_op jit(solution)/shard_map/ppermute | solution.py:132
  119.8 0.8 shard_map.41
  120.6 3.8 %all_to_all.40 = bf16[2,8,2,2,8,128]{5,4,3,2,1,0:T(8,128)(2,1)S(1)} all-to-all(bf16[2,8,2,2,8,128]{5,4,3,2,1,0:T(8,128)(2,1)S(1)} %bitcast.6), channel_id=1, replica_groups=mesh['zh'=4,'zl'=2,'x'=4,'y'=8,'core'=2] {'core'}, dimensions={0} | all-to-all | bytes 262144 | tf_op jit(solution)/shard_map/all_to_all | solution.py:180
  124.5 9.2 %all_to_all.41 = bf16[2,8,2,2,8,128]{5,4,3,2,0,1:T(8,128)(2,1)S(1)} all-to-all(bf16[2,8,2,2,8,128]{5,4,3,2,0,1:T(8,128)(2,1)S(1)} %copy.6), channel_id=1, replica_groups=mesh['zh'=4,'zl'=2,'x'=4,'y'=8,'core'=2] {'zl','x'}, dimensions={1} | all-to-all | bytes 262144 | tf_op jit(solution)/shard_map/all_to_all | solution.py:181
  133.6 0.9 shard_map.42
  (3 shorter events, 0.0 us)
Async XLA Ops:
  6.5 73.9 %all-gather.3.cloned.1.call-start = ((), (), s32[]{:S(2)}) async-start(), calls=%async_computation.7 | async-start | bytes 3538944 | tf_op jit(solution)/shard_map/all_gather | solution.py:143
  6.5 0.8 copy-start.3
  7.4 0.8 copy-start.4
  36.9 0.9 copy-start.2
  52.4 3.9 %collective-permute-start = (bf16[8,2,8,2304]{3,2,1,0:T(8,128)(2,1)S(1)}, bf16[8,2,8,2304]{3,2,1,0:T(8,128)(2,1)S(1)}, u32[]{:S(2)}, u32[]{:S(2)}) collective-permute-start(bf16[8,2,8,2304]{3,2,1,0:T(8,128)(2,1)S(1)} %all_to_all.37.own_ref), channel_id=1, source_target_pairs={{0,1},{1,0},{2,3},{3,2},{4,5},{5,4},{6,7},{7,6},{8,9},{9,8},{10,11... | collective-permute-start | bytes 1769480 | tf_op jit(solution)/shard_map/ppermute | solution.py:132
  80.5 1.9 %copy-start = (bf16[32,2,3,2,32,128]{5,4,3,2,1,0:T(8,128)(2,1)S(1)}, bf16[32,2,3,2,32,128]{5,4,3,2,1,0:T(8,128)(2,1)}, u32[]{:S(2)}) copy-start(bf16[32,2,3,2,32,128]{5,4,3,2,1,0:T(8,128)(2,1)} %all-gather.3.cloned.1.call-done) | copy-start | bytes 9437188
  82.4 19.8 %copy-start.1 = (bf16[32,2,3,2,32,128]{5,4,3,2,1,0:T(8,128)(2,1)S(1)}, bf16[32,2,3,2,32,128]{5,4,3,2,1,0:T(8,128)(2,1)}, u32[]{:S(2)}) copy-start(bf16[32,2,3,2,32,128]{5,4,3,2,1,0:T(8,128)(2,1)} %all-gather.3.cloned.1.call-done) | copy-start | bytes 9437188
  98.4 3.8 %collective-permute-start.1 = (bf16[8,2,128,128]{3,2,1,0:T(8,128)(2,1)S(1)}, bf16[8,2,128,128]{3,2,1,0:T(8,128)(2,1)S(1)}, u32[]{:S(2)}, u32[]{:S(2)}) collective-permute-start(bf16[8,2,128,128]{3,2,1,0:T(8,128)(2,1)S(1)} %all_to_all.38.own_ref), channel_id=1, source_target_pairs={{0,1},{1,0},{2,3},{3,2},{4,5},{5,4},{6,7},{7,6},{8,9},{9,8},{10,11... | collective-permute-start | bytes 1572872 | tf_op jit(solution)/shard_map/ppermute | solution.py:132
  116.0 3.8 %collective-permute-start.2 = (bf16[8,2,128,128]{3,2,1,0:T(8,128)(2,1)S(1)}, bf16[8,2,128,128]{3,2,1,0:T(8,128)(2,1)S(1)}, u32[]{:S(2)}, u32[]{:S(2)}) collective-permute-start(bf16[8,2,128,128]{3,2,1,0:T(8,128)(2,1)S(1)} %all_to_all.39.own_ref), channel_id=1, source_target_pairs={{0,1},{1,0},{2,3},{3,2},{4,5},{5,4},{6,7},{7,6},{8,9},{9,8},{10,11... | collective-permute-start | bytes 1572872 | tf_op jit(solution)/shard_map/ppermute | solution.py:132
Sparse Core Ops, SparseCore 0:
  37.0 43.4 all-gather.2

commit v2 on v0

v2 whole, which is shorter than its diff:
```python
import jax
import jax.numpy as jnp
from jax import lax
from jax.experimental import pallas as pl
from jax.experimental.pallas import tpu as pltpu
from jax.sharding import Mesh, PartitionSpec as P

F32, BF16 = jnp.float32, jnp.bfloat16
ZH, ZL, X, Y, CORES = 4, 2, 4, 8, 2
GROUP = ZL * X
PANEL, SHOTS = 2048, 8
ROWS = PANEL // GROUP
COLS = PANEL // Y
GROUP_SHOTS = GROUP * SHOTS
VMEM_BYTES = 40 * 1024 * 1024
VMEM = pl.BlockSpec(memory_space=pltpu.VMEM)
SMEM = pl.BlockSpec(memory_space=pltpu.SMEM)
NT = (((1,), (1,)), ((), ()))


def call(body, outs, *args, scalars=0, scratch=(), flops=0, moved=1 << 20):
    return pl.pallas_call(
        body,
        out_shape=outs,
        in_specs=[SMEM] * scalars + [VMEM] * (len(args) - scalars),
        out_specs=jax.tree.map(lambda _: VMEM, outs),
        scratch_shapes=list(scratch),
        compiler_params=pltpu.CompilerParams(vmem_limit_bytes=VMEM_BYTES),
        cost_estimate=pl.CostEstimate(flops=flops, bytes_accessed=moved, transcendentals=0),
    )(*args)


def array(*dims):
    return jax.ShapeDtypeStruct(dims, BF16)


def pack_fields(b_ref, cols_ref, rows_ref):
    for c in range(2):
        for y in range(Y):
            cols_ref[y, c] = b_ref[c, 0, :, y * COLS : y * COLS + COLS]
        for d in range(GROUP):
            parts = [b_ref[c, 1, :, zh * 512 + d * 64 : zh * 512 + d * 64 + 64] for zh in range(ZH)]
            rows_ref[d, c] = jnp.concatenate(parts, axis=-1)


def repeat_fields(cols_ref, rows_ref, out_ref):
    for d in range(GROUP):
        for y in range(Y):
            for c in range(2):
                out_ref[d, y * 2 + c] = cols_ref[y, c]
        for c in range(2):
            out_ref[d, 2 * Y + c] = rows_ref[d, c]


def pack_matrices(diag_ref, coup_ref, out_ref):
    for c in range(2):
        out_ref[0, c] = diag_ref[c, 0]
        out_ref[1, c] = coup_ref[c]
        out_ref[2, c] = diag_ref[c, 1]


def split_matrices(m0_ref, m1_ref, m2_ref, m3_ref, first_ref, rest_ref):
    for back, ref in enumerate((m0_ref, m1_ref, m2_ref, m3_ref)):
        for c in range(2):
            first_ref[back, c] = ref[0, c]
            rest_ref[back, 0, c] = ref[1, c]
            rest_ref[back, 1, c] = ref[2, c]


def row_of(zh, back, c):
    return pl.multiple_of(c * ROWS + lax.rem(zh - back + ZH, ZH) * 64, 64)


def complex_parts(prod):
    shots, rows = prod.shape[0] // 2, prod.shape[1] // 2
    real = prod[:shots, :rows] - prod[shots:, rows:]
    imag = prod[:shots, rows:] + prod[shots:, :rows]
    return real, imag


def first_partial(at_ref, v_ref, own_ref, other_ref, out_ref, slice_ref, mat_ref, vec_ref):
    core, zh = at_ref[0], at_ref[1]
    for ref, who in ((own_ref, core), (other_ref, 1 - core)):
        col = pl.multiple_of(who * 128, 128)
        for c in range(2):
            for back in range(ZH):
                mat_ref[pl.ds(row_of(zh, back, c), 64), pl.ds(col, 128)] = ref[back, c]
    for c in range(2):
        for y in range(Y):
            row = (c * Y + y) * GROUP_SHOTS
            block = v_ref[:, y * 2 + c].reshape(GROUP_SHOTS, COLS)
            vec_ref[row : row + GROUP_SHOTS, :] = block
        slice_ref[c] = v_ref[:, 2 * Y + c].reshape(GROUP_SHOTS, ROWS)
    prod = lax.dot_general(vec_ref[...], mat_ref[...], NT, preferred_element_type=F32)
    for c, part in enumerate(complex_parts(prod)):
        out_ref[:, c] = part.reshape(Y, GROUP_SHOTS, ROWS).astype(BF16)


def first_sum(parts_ref, rep_ref, first_ref):
    for c in range(2):
        total = parts_ref[0, c].astype(F32)
        for y in range(1, Y):
            total = total + parts_ref[y, c].astype(F32)
        total = total.astype(BF16)
        first_ref[c] = total
        for d in range(GROUP):
            rep_ref[d, c] = total


def product(at_ref, v_ref, m_ref, which, mat_ref, vec_ref):
    zh = at_ref[1]
    for y in range(Y):
        for core in range(CORES):
            col = (y * CORES + core) * 128
            for back in range(ZH):
                for c in range(2):
                    mat_ref[pl.ds(row_of(zh, back, c), 64), col : col + 128] = m_ref[
                        y * CORES + core, back, which, c
                    ]
    for c in range(2):
        for h in range(ZH):
            for d in range(0, GROUP, 2):
                pair = [v_ref[d + k, c, :, h * 64 : h * 64 + 64] for k in range(2)]
                col = h * 512 + d * 64
                rows = slice(c * GROUP_SHOTS, (c + 1) * GROUP_SHOTS)
                vec_ref[rows, col : col + 128] = jnp.concatenate(pair, axis=-1)
    prod = lax.dot_general(vec_ref[...], mat_ref[...], NT, preferred_element_type=F32)
    return complex_parts(prod)


def second_stage(at_ref, v_ref, m_ref, slice_ref, rep_ref, mat_ref, vec_ref):
    for c, part in enumerate(product(at_ref, v_ref, m_ref, 0, mat_ref, vec_ref)):
        residual = (slice_ref[c].astype(F32) - part).astype(BF16)
        for d in range(GROUP):
            rep_ref[d, c] = residual


def third_stage(at_ref, v_ref, m_ref, first_ref, out_ref, mat_ref, vec_ref):
    for c, part in enumerate(product(at_ref, v_ref, m_ref, 1, mat_ref, vec_ref)):
        out_ref[:, c, 0] = first_ref[c].reshape(GROUP, SHOTS, ROWS)
        out_ref[:, c, 1] = part.reshape(GROUP, SHOTS, ROWS).astype(BF16)


def unpack(in_ref, out_ref):
    for c in range(2):
        for p in range(2):
            for h in range(ZH):
                for d in range(0, GROUP, 2):
                    pair = [in_ref[d + k, c, p, :, h * 64 : h * 64 + 64] for k in range(2)]
                    col = h * 512 + d * 64
                    out_ref[c, p, :, col : col + 128] = jnp.concatenate(pair, axis=-1)


def exchange(block, axes):
    return lax.all_to_all(block, axes, 0, 0, tiled=True)


def shift(block, axis, size, by):
    return lax.ppermute(block, axis, [(i, (i + by) % size) for i in range(size)])


def on_device(shot_fields, diag_inverse, coupling):
    group = ("zl", "x")
    at = jnp.stack([lax.axis_index("core"), lax.axis_index("zh")])

    mats = call(pack_matrices, array(3, 2, 64, 128), diag_inverse, coupling)
    mats = [mats] + [shift(mats, "zh", ZH, by) for by in range(1, ZH)]
    first_mat, rest = call(
        split_matrices, (array(ZH, 2, 64, 128), array(ZH, 2, 2, 64, 128)), *mats
    )
    rest = lax.all_gather(rest, ("y", "core"), axis=0)
    first_mat = (first_mat, shift(first_mat, "core", CORES, 1))

    cols, rows = call(
        pack_fields, (array(Y, 2, SHOTS, COLS), array(GROUP, 2, SHOTS, ROWS)), shot_fields
    )
    cols = exchange(cols, "y")
    fields = call(repeat_fields, array(GROUP, 2 * Y + 2, SHOTS, COLS), cols, rows)
    fields = exchange(fields, group)

    block = array(2, GROUP_SHOTS, ROWS)
    repeated = array(GROUP, 2, GROUP_SHOTS, ROWS)
    parts, second_slice = call(
        first_partial,
        (array(Y, 2, GROUP_SHOTS, ROWS), block),
        at,
        fields,
        *first_mat,
        scalars=1,
        scratch=[pltpu.VMEM((2 * ROWS, COLS), BF16), pltpu.VMEM((2 * Y * GROUP_SHOTS, COLS), BF16)],
    )
    first_rep, first = call(first_sum, (repeated, block), exchange(parts, "y"))

    def stage(body, outs, *args):
        scratch = [pltpu.VMEM((2 * ROWS, PANEL), BF16), pltpu.VMEM((2 * GROUP_SHOTS, PANEL), BF16)]
        flops = 2 * 2 * ROWS * PANEL * 2 * GROUP_SHOTS
        return call(body, outs, at, *args, scalars=1, scratch=scratch, flops=flops, moved=3 << 20)

    residual = stage(second_stage, repeated, exchange(first_rep, group), rest, second_slice)
    both = stage(
        third_stage, array(GROUP, 2, 2, SHOTS, ROWS), exchange(residual, group), rest, first
    )
    return call(unpack, array(2, 2, SHOTS, PANEL), exchange(both, group))


def solution(mesh):
    axes = ("zh", "zl", "x", "y", "core")
    fine = Mesh(mesh.devices.reshape(ZH, ZL, X, Y, CORES), axes)
    row, src = axes[:3], axes[3:]
    in_specs = (
        P(None, None, row + src, None),
        P(None, None, row, src),
        P(None, row, src),
    )
    out_specs = P(None, None, row + src, None)
    return jax.shard_map(
        on_device, mesh=fine, in_specs=in_specs, out_specs=out_specs, check_vma=False
    )
```

time: 298 us -> 134 us (0.45)
  the two profiles are of different devices: /device:TPU:8 before, /device:TPU:2 now
where the time goes in v2:
time: 134 us; the launch traced here: 133 us
  blocking collectives  71.1 us (53%)
  starting transfers between devices  25.6 us (19%)
  between operations  13.5 us (10%)
  waiting for transfers between devices  11.2 us (8%)
  Pallas kernels  7.22 us (5%)
  local copies, waits for them, and re-layouts  4.69 us (4%)
    all_to_all x5, blocking collectives, exchange(): return lax.all_to_all(block, axes, 0, 0, tiled=True)  71.1 us
    ppermute x4, starting transfers between devices, shift(): lax.ppermute(block, axis, [(i, (i + by) % size) for i in range(size)])  20.8 us
    ppermute x4, waiting for transfers between devices, shift(): lax.ppermute(block, axis, [(i, (i + by) % size) for i in range(size)])  7.43 us
    pallas_call x9, Pallas kernels, call(): pl.pallas_call(body, out_shape=outs, in_specs=[SMEM] * scalars + [VMEM] *...  7.22 us
    all_to_all x1, starting transfers between devices, exchange(): return lax.all_to_all(block, axes, 0, 0, tiled=True)  4.83 us
    unnamed x10, local copies, waits for them, and re-layouts  4.69 us
    all_to_all x1, waiting for transfers between devices, exchange(): return lax.all_to_all(block, axes, 0, 0, tiled=True)  3.8 us
  transfers between devices with their start and end apart: 6, of which 4 were waited for; matrix products, arithmetic and copies ran while one was open for 0% of the time, Pallas kernels for 2%

profile of v2, /device:TPU:2, one launch (start us, length us, event | category | flops | bytes accessed | tf_op | source)
XLA Modules:
  0.0 133.4 jit_solution(15905598440899495799)
XLA Ops:
  6.5 0.0 all-gather.3.cloned.1.call-start
  6.5 0.0 copy-start.3
  6.5 0.8 copy-done.3
  7.4 0.0 copy-start.4
  7.4 0.8 copy-done.4
  8.1 6.1 %collective-permute-start = (bf16[3,2,64,128]{3,2,1,0:T(8,128)(2,1)S(1)}, bf16[3,2,64,128]{3,2,1,0:T(8,128)(2,1)S(1)}, u32[]{:S(2)}, u32[]{:S(2)}) collective-permute-start(bf16[3,2,64,128]{3,2,1,0:T(8,128)(2,1)S(1)} %shard_map.39.m0_ref), channel_id=1, source_target_pairs={{0,128},{128,256},{256,384},{384,0},{1,129},{129,257},{257,385},{3... | collective-permute-start | bytes 294920 | tf_op jit(solution)/shard_map/ppermute | solution.py:159
  14.2 9.1 %collective-permute-start.1 = (bf16[3,2,64,128]{3,2,1,0:T(8,128)(2,1)S(1)}, bf16[3,2,64,128]{3,2,1,0:T(8,128)(2,1)S(1)}, u32[]{:S(2)}, u32[]{:S(2)}) collective-permute-start(bf16[3,2,64,128]{3,2,1,0:T(8,128)(2,1)S(1)} %shard_map.39.m0_ref), channel_id=1, source_target_pairs={{0,256},{128,384},{256,0},{384,128},{1,257},{129,385},{257,1},{385... | collective-permute-start | bytes 294920 | tf_op jit(solution)/shard_map/ppermute | solution.py:159
  23.4 3.7 %collective-permute-start.2 = (bf16[3,2,64,128]{3,2,1,0:T(8,128)(2,1)S(1)}, bf16[3,2,64,128]{3,2,1,0:T(8,128)(2,1)S(1)}, u32[]{:S(2)}, u32[]{:S(2)}) collective-permute-start(bf16[3,2,64,128]{3,2,1,0:T(8,128)(2,1)S(1)} %shard_map.39.m0_ref), channel_id=1, source_target_pairs={{0,384},{128,0},{256,128},{384,256},{1,385},{129,1},{257,129},{385... | collective-permute-start | bytes 294920 | tf_op jit(solution)/shard_map/ppermute | solution.py:159
  27.0 0.0 collective-permute-done.m1_ref
  27.0 2.9 %collective-permute-done.1.m2_ref = bf16[3,2,64,128]{3,2,1,0:T(8,128)(2,1)S(1)} collective-permute-done((bf16[3,2,64,128]{3,2,1,0:T(8,128)(2,1)S(1)}, bf16[3,2,64,128]{3,2,1,0:T(8,128)(2,1)S(1)}, u32[]{:S(2)}, u32[]{:S(2)}) %collective-permute-start.1) | collective-permute-done | bytes 98336 | tf_op jit(solution)/shard_map/ppermute | solution.py:159
  29.9 3.3 %collective-permute-done.2.m3_ref = bf16[3,2,64,128]{3,2,1,0:T(8,128)(2,1)S(1)} collective-permute-done((bf16[3,2,64,128]{3,2,1,0:T(8,128)(2,1)S(1)}, bf16[3,2,64,128]{3,2,1,0:T(8,128)(2,1)S(1)}, u32[]{:S(2)}, u32[]{:S(2)}) %collective-permute-start.2) | collective-permute-done | bytes 98336 | tf_op jit(solution)/shard_map/ppermute | solution.py:159
  33.2 0.7 shard_map.40
  34.0 0.0 all-gather.3.cloned.1.call-update
  34.0 0.0 copy-start.2
  34.0 0.9 copy-done.2
  34.9 0.1 shard_map.37
  35.0 15.3 %all_to_all.30.cols_ref = bf16[8,2,8,256]{3,2,1,0:T(8,128)(2,1)S(1)} all-to-all(bf16[8,2,8,256]{3,2,1,0:T(8,128)(2,1)S(1)} %get-tuple-element.13), channel_id=1, replica_groups=mesh['zh'=4,'zl'=2,'x'=4,'y'=8,'core'=2] {'y'}, dimensions={0} | all-to-all | bytes 131072 | tf_op jit(solution)/shard_map/all_to_all | solution.py:155
  50.3 0.9 shard_map.38
  51.1 4.8 %all-to-all-start.1 = ((bf16[8,18,8,256]{3,2,1,0:T(8,128)(2,1)}), bf16[8,18,8,256]{3,2,1,0:T(8,128)(2,1)S(1)}, u32[]{:S(2)}, u32[]{:S(2)}) async-start(bf16[8,18,8,256]{3,2,1,0:T(8,128)(2,1)} %shard_map.38), calls=%async_computation.1 | async-start | bytes 1179648 | tf_op jit(solution)/shard_map/all_to_all | solution.py:155
  56.0 1.9 %collective-permute-start.3 = (bf16[4,2,64,128]{3,2,1,0:T(8,128)(2,1)S(1)}, bf16[4,2,64,128]{3,2,1,0:T(8,128)(2,1)S(1)}, u32[]{:S(2)}, u32[]{:S(2)}) collective-permute-start(bf16[4,2,64,128]{3,2,1,0:T(8,128)(2,1)S(1)} %get-tuple-element.15.own_ref), channel_id=1, source_target_pairs={{0,1},{1,0},{2,3},{3,2},{4,5},{5,4},{6,7},{7,6},{8,9},{9,8},{10,11... | collective-permute-start | bytes 393224 | tf_op jit(solution)/shard_map/ppermute | solution.py:159
  57.9 0.1 pad_add_fusion.at_ref
  58.0 1.2 collective-permute-done.3.other_ref
  59.2 3.8 %all-to-all-done.1.v_ref = bf16[8,18,8,256]{3,2,1,0:T(8,128)(2,1)S(1)} async-done(((bf16[8,18,8,256]{3,2,1,0:T(8,128)(2,1)}), bf16[8,18,8,256]{3,2,1,0:T(8,128)(2,1)S(1)}, u32[]{:S(2)}, u32[]{:S(2)}) %all-to-all-start.1) | async-done | bytes 589856 | tf_op jit(solution)/shard_map/all_to_all | solution.py:155
  63.0 1.1 shard_map.41
  64.1 22.9 %all_to_all.31.parts_ref = bf16[8,2,64,256]{3,2,1,0:T(8,128)(2,1)S(1)} all-to-all(bf16[8,2,64,256]{3,2,1,0:T(8,128)(2,1)S(1)} %get-tuple-element.16), channel_id=1, replica_groups=mesh['zh'=4,'zl'=2,'x'=4,'y'=8,'core'=2] {'y'}, dimensions={0} | all-to-all | bytes 1048576 | tf_op jit(solution)/shard_map/all_to_all | solution.py:155
  87.0 0.1 shard_map.42
  87.0 12.2 %all_to_all.32.v_ref = bf16[8,2,64,256]{3,2,1,0:T(8,128)(2,1)S(1)} all-to-all(bf16[8,2,64,256]{3,2,1,0:T(8,128)(2,1)S(1)} %get-tuple-element.17), channel_id=1, replica_groups=mesh['zh'=4,'zl'=2,'x'=4,'y'=8,'core'=2] {'zl','x'}, dimensions={0} | all-to-all | bytes 1048576 | tf_op jit(solution)/shard_map/all_to_all | solution.py:155
  99.3 0.0 all-gather.3.cloned.1.call-done
  99.3 0.0 copy-start
  99.3 2.2 %copy-done = bf16[64,2,2,64,128]{4,3,2,1,0:T(8,128)(2,1)S(1)} copy-done((bf16[64,2,2,64,128]{4,3,2,1,0:T(8,128)(2,1)S(1)}, bf16[64,2,2,64,128]{4,3,2,1,0:T(8,128)(2,1)}, u32[]{:S(2)}) %copy-start) | copy-done | bytes 4194328
  101.5 0.0 copy-start.1
  101.5 1.8 %shard_map.43 = bf16[8,2,64,256]{3,2,1,0:T(8,128)(2,1)S(1)} custom-call(s32[2]{0:T(128)S(1)} %pad_add_fusion.at_ref, bf16[8,2,64,256]{3,2,1,0:T(8,128)(2,1)S(1)} %all_to_all.32.v_ref, bf16[16,4,2,2,64,128]{5,4,3,2,1,0:T(8,128)(2,1)S(1)} %bitcast.3, bf16[2,64,256]{2,1,0:T(8,128)(2,1)S(1)} %get-tuple-element.19.slice_ref), custom_call_target="tpu_custom_call" | custom-call | flops 268435456 | bytes 3145728 | tf_op jit(solution)/shard_map/pallas_call | solution.py:22
  103.3 11.2 %all_to_all.33.v_ref = bf16[8,2,64,256]{3,2,1,0:T(8,128)(2,1)S(1)} all-to-all(bf16[8,2,64,256]{3,2,1,0:T(8,128)(2,1)S(1)} %shard_map.43), channel_id=1, replica_groups=mesh['zh'=4,'zl'=2,'x'=4,'y'=8,'core'=2] {'zl','x'}, dimensions={0} | all-to-all | bytes 1048576 | tf_op jit(solution)/shard_map/all_to_all | solution.py:155
  114.5 0.0 copy-done.1
  114.5 1.8 %shard_map.44 = bf16[8,2,2,8,256]{4,3,2,1,0:T(8,128)(2,1)S(1)} custom-call(s32[2]{0:T(128)S(1)} %pad_add_fusion.at_ref, bf16[8,2,64,256]{3,2,1,0:T(8,128)(2,1)S(1)} %all_to_all.33.v_ref, bf16[16,4,2,2,64,128]{5,4,3,2,1,0:T(8,128)(2,1)S(1)} %bitcast.4, bf16[2,64,256]{2,1,0:T(8,128)(2,1)S(1)} %get-tuple-element.20.first_ref), custom_call_target="tpu_custom_call" | custom-call | flops 268435456 | bytes 3145728 | tf_op jit(solution)/shard_map/pallas_call | solution.py:22
  116.3 9.5 %all_to_all.34.in_ref = bf16[8,2,2,8,256]{4,3,2,1,0:T(8,128)(2,1)S(1)} all-to-all(bf16[8,2,2,8,256]{4,3,2,1,0:T(8,128)(2,1)S(1)} %shard_map.44), channel_id=1, replica_groups=mesh['zh'=4,'zl'=2,'x'=4,'y'=8,'core'=2] {'zl','x'}, dimensions={0} | all-to-all | bytes 262144 | tf_op jit(solution)/shard_map/all_to_all | solution.py:155
  125.8 0.8 shard_map.45
  (1 shorter events, 0.0 us)
Async XLA Ops:
  6.5 92.7 %all-gather.3.cloned.1.call-start = ((), (), s32[]{:S(2)}) async-start(), calls=%async_computation.6 | async-start | bytes 4456448 | tf_op jit(solution)/shard_map/all_gather | solution.py:171
  6.5 0.8 copy-start.3
  7.4 0.8 copy-start.4
  8.1 18.9 %collective-permute-start = (bf16[3,2,64,128]{3,2,1,0:T(8,128)(2,1)S(1)}, bf16[3,2,64,128]{3,2,1,0:T(8,128)(2,1)S(1)}, u32[]{:S(2)}, u32[]{:S(2)}) collective-permute-start(bf16[3,2,64,128]{3,2,1,0:T(8,128)(2,1)S(1)} %shard_map.39.m0_ref), channel_id=1, source_target_pairs={{0,128},{128,256},{256,384},{384,0},{1,129},{129,257},{257,385},{3... | collective-permute-start | bytes 294920 | tf_op jit(solution)/shard_map/ppermute | solution.py:159
  14.2 15.7 %collective-permute-start.1 = (bf16[3,2,64,128]{3,2,1,0:T(8,128)(2,1)S(1)}, bf16[3,2,64,128]{3,2,1,0:T(8,128)(2,1)S(1)}, u32[]{:S(2)}, u32[]{:S(2)}) collective-permute-start(bf16[3,2,64,128]{3,2,1,0:T(8,128)(2,1)S(1)} %shard_map.39.m0_ref), channel_id=1, source_target_pairs={{0,256},{128,384},{256,0},{384,128},{1,257},{129,385},{257,1},{385... | collective-permute-start | bytes 294920 | tf_op jit(solution)/shard_map/ppermute | solution.py:159
  23.4 9.9 %collective-permute-start.2 = (bf16[3,2,64,128]{3,2,1,0:T(8,128)(2,1)S(1)}, bf16[3,2,64,128]{3,2,1,0:T(8,128)(2,1)S(1)}, u32[]{:S(2)}, u32[]{:S(2)}) collective-permute-start(bf16[3,2,64,128]{3,2,1,0:T(8,128)(2,1)S(1)} %shard_map.39.m0_ref), channel_id=1, source_target_pairs={{0,384},{128,0},{256,128},{384,256},{1,385},{129,1},{257,129},{385... | collective-permute-start | bytes 294920 | tf_op jit(solution)/shard_map/ppermute | solution.py:159
  34.0 0.9 copy-start.2
  51.1 11.9 %all-to-all-start.1 = ((bf16[8,18,8,256]{3,2,1,0:T(8,128)(2,1)}), bf16[8,18,8,256]{3,2,1,0:T(8,128)(2,1)S(1)}, u32[]{:S(2)}, u32[]{:S(2)}) async-start(bf16[8,18,8,256]{3,2,1,0:T(8,128)(2,1)} %shard_map.38), calls=%async_computation.1 | async-start | bytes 1179648 | tf_op jit(solution)/shard_map/all_to_all | solution.py:155
  56.0 3.2 %collective-permute-start.3 = (bf16[4,2,64,128]{3,2,1,0:T(8,128)(2,1)S(1)}, bf16[4,2,64,128]{3,2,1,0:T(8,128)(2,1)S(1)}, u32[]{:S(2)}, u32[]{:S(2)}) collective-permute-start(bf16[4,2,64,128]{3,2,1,0:T(8,128)(2,1)S(1)} %get-tuple-element.15.own_ref), channel_id=1, source_target_pairs={{0,1},{1,0},{2,3},{3,2},{4,5},{5,4},{6,7},{7,6},{8,9},{9,8},{10,11... | collective-permute-start | bytes 393224 | tf_op jit(solution)/shard_map/ppermute | solution.py:159
  99.3 2.2 %copy-start = (bf16[64,2,2,64,128]{4,3,2,1,0:T(8,128)(2,1)S(1)}, bf16[64,2,2,64,128]{4,3,2,1,0:T(8,128)(2,1)}, u32[]{:S(2)}) copy-start(bf16[64,2,2,64,128]{4,3,2,1,0:T(8,128)(2,1)} %all-gather.3.cloned.1.call-done) | copy-start | bytes 12582916
  101.5 13.0 %copy-start.1 = (bf16[64,2,2,64,128]{4,3,2,1,0:T(8,128)(2,1)S(1)}, bf16[64,2,2,64,128]{4,3,2,1,0:T(8,128)(2,1)}, u32[]{:S(2)}) copy-start(bf16[64,2,2,64,128]{4,3,2,1,0:T(8,128)(2,1)} %all-gather.3.cloned.1.call-done) | copy-start | bytes 12582916
Sparse Core Ops, SparseCore 0:
  34.1 51.3 all-gather.2

commit v3 on v2

--- a/solution.py
+++ b/solution.py
@@ -163,18 +163,18 @@
     group = ("zl", "x")
     at = jnp.stack([lax.axis_index("core"), lax.axis_index("zh")])
 
+    cols, rows = call(
+        pack_fields, (array(Y, 2, SHOTS, COLS), array(GROUP, 2, SHOTS, ROWS)), shot_fields
+    )
     mats = call(pack_matrices, array(3, 2, 64, 128), diag_inverse, coupling)
-    mats = [mats] + [shift(mats, "zh", ZH, by) for by in range(1, ZH)]
+    cols, mats = lax.optimization_barrier((cols, mats))
+    moved = [shift(mats, "zh", ZH, by) for by in range(1, ZH)]
+    cols, *moved = lax.optimization_barrier((exchange(cols, "y"), *moved))
     first_mat, rest = call(
-        split_matrices, (array(ZH, 2, 64, 128), array(ZH, 2, 2, 64, 128)), *mats
+        split_matrices, (array(ZH, 2, 64, 128), array(ZH, 2, 2, 64, 128)), mats, *moved
     )
     rest = lax.all_gather(rest, ("y", "core"), axis=0)
     first_mat = (first_mat, shift(first_mat, "core", CORES, 1))
-
-    cols, rows = call(
-        pack_fields, (array(Y, 2, SHOTS, COLS), array(GROUP, 2, SHOTS, ROWS)), shot_fields
-    )
-    cols = exchange(cols, "y")
     fields = call(repeat_fields, array(GROUP, 2 * Y + 2, SHOTS, COLS), cols, rows)
     fields = exchange(fields, group)
 

time: 134 us -> 134 us (level)
  the two profiles are of different devices: /device:TPU:2 before, /device:TPU:8 now
where the time goes in v3:
time: 134 us; the launch traced here: 133 us
  blocking collectives  62 us (46%)
  starting transfers between devices  32.6 us (24%)
  between operations  13.5 us (10%)
  waiting for transfers between devices  12.8 us (10%)
  Pallas kernels  7.76 us (6%)
  local copies, waits for them, and re-layouts  4.69 us (4%)
    all_to_all x4, blocking collectives, exchange(): return lax.all_to_all(block, axes, 0, 0, tiled=True)  62 us
    ppermute x4, starting transfers between devices, shift(): lax.ppermute(block, axis, [(i, (i + by) % size) for i in range(size)])  19.2 us
    all_to_all x2, starting transfers between devices, exchange(): return lax.all_to_all(block, axes, 0, 0, tiled=True)  13.4 us
    pallas_call x9, Pallas kernels, call(): pl.pallas_call(body, out_shape=outs, in_specs=[SMEM] * scalars + [VMEM] *...  7.76 us
    ppermute x4, waiting for transfers between devices, shift(): lax.ppermute(block, axis, [(i, (i + by) % size) for i in range(size)])  6.87 us
    all_to_all x2, waiting for transfers between devices, exchange(): return lax.all_to_all(block, axes, 0, 0, tiled=True)  5.88 us
    unnamed x10, local copies, waits for them, and re-layouts  4.69 us
  transfers between devices with their start and end apart: 7, of which 4 were waited for; matrix products, arithmetic and copies ran while one was open for 0% of the time, Pallas kernels for 2%

profile of v3, /device:TPU:8, one launch (start us, length us, event | category | flops | bytes accessed | tf_op | source)
XLA Modules:
  0.0 133.4 jit_solution(5258238544791757053)
XLA Ops:
  6.5 0.0 copy-start.2
  6.5 0.9 copy-done.2
  7.4 0.6 shard_map.37
  8.1 0.0 copy-start.3
  8.1 0.8 copy-done.3
  8.9 0.0 copy-start.4
  8.9 0.8 copy-done.4
  9.7 9.1 %all-to-all-start = ((bf16[8,2,8,256]{3,2,1,0:T(8,128)(2,1)}), bf16[8,2,8,256]{3,2,1,0:T(8,128)(2,1)S(1)}, u32[]{:S(2)}, u32[]{:S(2)}) async-start(bf16[8,2,8,256]{3,2,1,0:T(8,128)(2,1)} %get-tuple-element.20), calls=%async_computation | async-start | bytes 131072 | tf_op jit(solution)/shard_map/all_to_all | solution.py:155
  18.8 0.0 all-gather.3.cloned.1.call-start
  18.8 4.5 %collective-permute-start = (bf16[3,2,64,128]{3,2,1,0:T(8,128)(2,1)S(1)}, bf16[3,2,64,128]{3,2,1,0:T(8,128)(2,1)S(1)}, u32[]{:S(2)}, u32[]{:S(2)}) collective-permute-start(bf16[3,2,64,128]{3,2,1,0:T(8,128)(2,1)S(1)} %shard_map.38.m0_ref), channel_id=1, source_target_pairs={{0,128},{128,256},{256,384},{384,0},{1,129},{129,257},{257,385},{3... | collective-permute-start | bytes 294920 | tf_op jit(solution)/shard_map/ppermute | solution.py:159
  23.3 9.1 %collective-permute-start.1 = (bf16[3,2,64,128]{3,2,1,0:T(8,128)(2,1)S(1)}, bf16[3,2,64,128]{3,2,1,0:T(8,128)(2,1)S(1)}, u32[]{:S(2)}, u32[]{:S(2)}) collective-permute-start(bf16[3,2,64,128]{3,2,1,0:T(8,128)(2,1)S(1)} %shard_map.38.m0_ref), channel_id=1, source_target_pairs={{0,256},{128,384},{256,0},{384,128},{1,257},{129,385},{257,1},{385... | collective-permute-start | bytes 294920 | tf_op jit(solution)/shard_map/ppermute | solution.py:159
  32.5 3.7 %collective-permute-start.2 = (bf16[3,2,64,128]{3,2,1,0:T(8,128)(2,1)S(1)}, bf16[3,2,64,128]{3,2,1,0:T(8,128)(2,1)S(1)}, u32[]{:S(2)}, u32[]{:S(2)}) collective-permute-start(bf16[3,2,64,128]{3,2,1,0:T(8,128)(2,1)S(1)} %shard_map.38.m0_ref), channel_id=1, source_target_pairs={{0,384},{128,0},{256,128},{384,256},{1,385},{129,1},{257,129},{385... | collective-permute-start | bytes 294920 | tf_op jit(solution)/shard_map/ppermute | solution.py:159
  36.1 0.0 collective-permute-done.m1_ref
  36.1 2.3 %collective-permute-done.1.m2_ref = bf16[3,2,64,128]{3,2,1,0:T(8,128)(2,1)S(1)} collective-permute-done((bf16[3,2,64,128]{3,2,1,0:T(8,128)(2,1)S(1)}, bf16[3,2,64,128]{3,2,1,0:T(8,128)(2,1)S(1)}, u32[]{:S(2)}, u32[]{:S(2)}) %collective-permute-start.1) | collective-permute-done | bytes 98336 | tf_op jit(solution)/shard_map/ppermute | solution.py:159
  38.4 3.4 %collective-permute-done.2.m3_ref = bf16[3,2,64,128]{3,2,1,0:T(8,128)(2,1)S(1)} collective-permute-done((bf16[3,2,64,128]{3,2,1,0:T(8,128)(2,1)S(1)}, bf16[3,2,64,128]{3,2,1,0:T(8,128)(2,1)S(1)}, u32[]{:S(2)}, u32[]{:S(2)}) %collective-permute-start.2) | collective-permute-done | bytes 98336 | tf_op jit(solution)/shard_map/ppermute | solution.py:159
  41.8 0.0 all-to-all-done.cols_ref
  41.8 0.7 shard_map.40
  42.5 0.0 all-gather.3.cloned.1.call-update
  42.5 0.9 shard_map.39
  43.4 4.3 %all-to-all-start.1 = ((bf16[8,18,8,256]{3,2,1,0:T(8,128)(2,1)}), bf16[8,18,8,256]{3,2,1,0:T(8,128)(2,1)S(1)}, u32[]{:S(2)}, u32[]{:S(2)}) async-start(bf16[8,18,8,256]{3,2,1,0:T(8,128)(2,1)} %shard_map.39), calls=%async_computation.1 | async-start | bytes 1179648 | tf_op jit(solution)/shard_map/all_to_all | solution.py:155
  47.7 1.9 %collective-permute-start.3 = (bf16[4,2,64,128]{3,2,1,0:T(8,128)(2,1)S(1)}, bf16[4,2,64,128]{3,2,1,0:T(8,128)(2,1)S(1)}, u32[]{:S(2)}, u32[]{:S(2)}) collective-permute-start(bf16[4,2,64,128]{3,2,1,0:T(8,128)(2,1)S(1)} %get-tuple-element.27.own_ref), channel_id=1, source_target_pairs={{0,1},{1,0},{2,3},{3,2},{4,5},{5,4},{6,7},{7,6},{8,9},{9,8},{10,11... | collective-permute-start | bytes 393224 | tf_op jit(solution)/shard_map/ppermute | solution.py:159
  49.6 0.1 pad_add_fusion.at_ref
  49.7 1.2 collective-permute-done.3.other_ref
  50.9 5.9 %all-to-all-done.1.v_ref = bf16[8,18,8,256]{3,2,1,0:T(8,128)(2,1)S(1)} async-done(((bf16[8,18,8,256]{3,2,1,0:T(8,128)(2,1)}), bf16[8,18,8,256]{3,2,1,0:T(8,128)(2,1)S(1)}, u32[]{:S(2)}, u32[]{:S(2)}) %all-to-all-start.1) | async-done | bytes 589856 | tf_op jit(solution)/shard_map/all_to_all | solution.py:155
  56.8 1.1 shard_map.41
  57.9 27.5 %all_to_all.30.parts_ref = bf16[8,2,64,256]{3,2,1,0:T(8,128)(2,1)S(1)} all-to-all(bf16[8,2,64,256]{3,2,1,0:T(8,128)(2,1)S(1)} %get-tuple-element.28), channel_id=1, replica_groups=mesh['zh'=4,'zl'=2,'x'=4,'y'=8,'core'=2] {'y'}, dimensions={0} | all-to-all | bytes 1048576 | tf_op jit(solution)/shard_map/all_to_all | solution.py:155
  85.4 0.1 shard_map.42
  85.5 12.7 %all_to_all.31.v_ref = bf16[8,2,64,256]{3,2,1,0:T(8,128)(2,1)S(1)} all-to-all(bf16[8,2,64,256]{3,2,1,0:T(8,128)(2,1)S(1)} %get-tuple-element.29), channel_id=1, replica_groups=mesh['zh'=4,'zl'=2,'x'=4,'y'=8,'core'=2] {'zl','x'}, dimensions={0} | all-to-all | bytes 1048576 | tf_op jit(solution)/shard_map/all_to_all | solution.py:155
  98.3 0.0 all-gather.3.cloned.1.call-done
  98.3 0.0 copy-start
  98.3 2.2 %copy-done = bf16[64,2,2,64,128]{4,3,2,1,0:T(8,128)(2,1)S(1)} copy-done((bf16[64,2,2,64,128]{4,3,2,1,0:T(8,128)(2,1)S(1)}, bf16[64,2,2,64,128]{4,3,2,1,0:T(8,128)(2,1)}, u32[]{:S(2)}) %copy-start) | copy-done | bytes 4194328
  100.4 0.0 copy-start.1
  100.4 1.8 %shard_map.43 = bf16[8,2,64,256]{3,2,1,0:T(8,128)(2,1)S(1)} custom-call(s32[2]{0:T(128)S(1)} %pad_add_fusion.at_ref, bf16[8,2,64,256]{3,2,1,0:T(8,128)(2,1)S(1)} %all_to_all.31.v_ref, bf16[16,4,2,2,64,128]{5,4,3,2,1,0:T(8,128)(2,1)S(1)} %bitcast.3, bf16[2,64,256]{2,1,0:T(8,128)(2,1)S(1)} %get-tuple-element.31.slice_ref), custom_call_target="tpu_custom_call" | custom-call | flops 268435456 | bytes 3145728 | tf_op jit(solution)/shard_map/pallas_call | solution.py:22
  102.3 12.6 %all_to_all.32.v_ref = bf16[8,2,64,256]{3,2,1,0:T(8,128)(2,1)S(1)} all-to-all(bf16[8,2,64,256]{3,2,1,0:T(8,128)(2,1)S(1)} %shard_map.43), channel_id=1, replica_groups=mesh['zh'=4,'zl'=2,'x'=4,'y'=8,'core'=2] {'zl','x'}, dimensions={0} | all-to-all | bytes 1048576 | tf_op jit(solution)/shard_map/all_to_all | solution.py:155
  114.9 0.0 copy-done.1
  114.9 1.8 %shard_map.44 = bf16[8,2,2,8,256]{4,3,2,1,0:T(8,128)(2,1)S(1)} custom-call(s32[2]{0:T(128)S(1)} %pad_add_fusion.at_ref, bf16[8,2,64,256]{3,2,1,0:T(8,128)(2,1)S(1)} %all_to_all.32.v_ref, bf16[16,4,2,2,64,128]{5,4,3,2,1,0:T(8,128)(2,1)S(1)} %bitcast.4, bf16[2,64,256]{2,1,0:T(8,128)(2,1)S(1)} %get-tuple-element.32.first_ref), custom_call_target="tpu_custom_call" | custom-call | flops 268435456 | bytes 3145728 | tf_op jit(solution)/shard_map/pallas_call | solution.py:22
  116.7 9.1 %all_to_all.33.in_ref = bf16[8,2,2,8,256]{4,3,2,1,0:T(8,128)(2,1)S(1)} all-to-all(bf16[8,2,2,8,256]{4,3,2,1,0:T(8,128)(2,1)S(1)} %shard_map.44), channel_id=1, replica_groups=mesh['zh'=4,'zl'=2,'x'=4,'y'=8,'core'=2] {'zl','x'}, dimensions={0} | all-to-all | bytes 262144 | tf_op jit(solution)/shard_map/all_to_all | solution.py:155
  125.8 0.8 shard_map.45
  (1 shorter events, 0.0 us)
Async XLA Ops:
  6.5 0.9 copy-start.2
  8.1 0.8 copy-start.3
  8.9 0.8 copy-start.4
  9.7 32.1 %all-to-all-start = ((bf16[8,2,8,256]{3,2,1,0:T(8,128)(2,1)}), bf16[8,2,8,256]{3,2,1,0:T(8,128)(2,1)S(1)}, u32[]{:S(2)}, u32[]{:S(2)}) async-start(bf16[8,2,8,256]{3,2,1,0:T(8,128)(2,1)} %get-tuple-element.20), calls=%async_computation | async-start | bytes 131072 | tf_op jit(solution)/shard_map/all_to_all | solution.py:155
  18.8 79.5 %all-gather.3.cloned.1.call-start = ((), (), s32[]{:S(2)}) async-start(), calls=%async_computation.6 | async-start | bytes 4456448 | tf_op jit(solution)/shard_map/all_gather | solution.py:176
  18.8 17.4 %collective-permute-start = (bf16[3,2,64,128]{3,2,1,0:T(8,128)(2,1)S(1)}, bf16[3,2,64,128]{3,2,1,0:T(8,128)(2,1)S(1)}, u32[]{:S(2)}, u32[]{:S(2)}) collective-permute-start(bf16[3,2,64,128]{3,2,1,0:T(8,128)(2,1)S(1)} %shard_map.38.m0_ref), channel_id=1, source_target_pairs={{0,128},{128,256},{256,384},{384,0},{1,129},{129,257},{257,385},{3... | collective-permute-start | bytes 294920 | tf_op jit(solution)/shard_map/ppermute | solution.py:159
  23.3 15.1 %collective-permute-start.1 = (bf16[3,2,64,128]{3,2,1,0:T(8,128)(2,1)S(1)}, bf16[3,2,64,128]{3,2,1,0:T(8,128)(2,1)S(1)}, u32[]{:S(2)}, u32[]{:S(2)}) collective-permute-start(bf16[3,2,64,128]{3,2,1,0:T(8,128)(2,1)S(1)} %shard_map.38.m0_ref), channel_id=1, source_target_pairs={{0,256},{128,384},{256,0},{384,128},{1,257},{129,385},{257,1},{385... | collective-permute-start | bytes 294920 | tf_op jit(solution)/shard_map/ppermute | solution.py:159
  32.5 9.3 %collective-permute-start.2 = (bf16[3,2,64,128]{3,2,1,0:T(8,128)(2,1)S(1)}, bf16[3,2,64,128]{3,2,1,0:T(8,128)(2,1)S(1)}, u32[]{:S(2)}, u32[]{:S(2)}) collective-permute-start(bf16[3,2,64,128]{3,2,1,0:T(8,128)(2,1)S(1)} %shard_map.38.m0_ref), channel_id=1, source_target_pairs={{0,384},{128,0},{256,128},{384,256},{1,385},{129,1},{257,129},{385... | collective-permute-start | bytes 294920 | tf_op jit(solution)/shard_map/ppermute | solution.py:159
  43.4 13.4 %all-to-all-start.1 = ((bf16[8,18,8,256]{3,2,1,0:T(8,128)(2,1)}), bf16[8,18,8,256]{3,2,1,0:T(8,128)(2,1)S(1)}, u32[]{:S(2)}, u32[]{:S(2)}) async-start(bf16[8,18,8,256]{3,2,1,0:T(8,128)(2,1)} %shard_map.39), calls=%async_computation.1 | async-start | bytes 1179648 | tf_op jit(solution)/shard_map/all_to_all | solution.py:155
  47.7 3.2 %collective-permute-start.3 = (bf16[4,2,64,128]{3,2,1,0:T(8,128)(2,1)S(1)}, bf16[4,2,64,128]{3,2,1,0:T(8,128)(2,1)S(1)}, u32[]{:S(2)}, u32[]{:S(2)}) collective-permute-start(bf16[4,2,64,128]{3,2,1,0:T(8,128)(2,1)S(1)} %get-tuple-element.27.own_ref), channel_id=1, source_target_pairs={{0,1},{1,0},{2,3},{3,2},{4,5},{5,4},{6,7},{7,6},{8,9},{9,8},{10,11... | collective-permute-start | bytes 393224 | tf_op jit(solution)/shard_map/ppermute | solution.py:159
  98.3 2.2 %copy-start = (bf16[64,2,2,64,128]{4,3,2,1,0:T(8,128)(2,1)S(1)}, bf16[64,2,2,64,128]{4,3,2,1,0:T(8,128)(2,1)}, u32[]{:S(2)}) copy-start(bf16[64,2,2,64,128]{4,3,2,1,0:T(8,128)(2,1)} %all-gather.3.cloned.1.call-done) | copy-start | bytes 12582916
  100.4 14.4 %copy-start.1 = (bf16[64,2,2,64,128]{4,3,2,1,0:T(8,128)(2,1)S(1)}, bf16[64,2,2,64,128]{4,3,2,1,0:T(8,128)(2,1)}, u32[]{:S(2)}) copy-start(bf16[64,2,2,64,128]{4,3,2,1,0:T(8,128)(2,1)} %all-gather.3.cloned.1.call-done) | copy-start | bytes 12582916
Sparse Core Ops, SparseCore 0:
  42.6 52.0 all-gather.2

commit v4 on v0

v4 whole, which is shorter than its diff:
```python
import jax
import jax.numpy as jnp
from jax import lax
from jax.experimental import pallas as pl
from jax.experimental.pallas import tpu as pltpu
from jax.sharding import Mesh, PartitionSpec as P

F32, BF16 = jnp.float32, jnp.bfloat16
ZH, ZL, X, Y, CORES = 4, 2, 4, 8, 2
SRC = Y * CORES
GROUP = ZL * X
PANEL, SHOTS = 2048, 8
ROWS = PANEL // GROUP
GROUP_SHOTS = GROUP * SHOTS
VMEM_BYTES = 40 * 1024 * 1024
VMEM = pl.BlockSpec(memory_space=pltpu.VMEM)
NT = (((1,), (1,)), ((), ()))


def call(body, outs, *args, scratch=(), flops=0, moved=1 << 20):
    return pl.pallas_call(
        body,
        out_shape=outs,
        in_specs=[VMEM] * len(args),
        out_specs=jax.tree.map(lambda _: VMEM, outs),
        scratch_shapes=list(scratch),
        compiler_params=pltpu.CompilerParams(vmem_limit_bytes=VMEM_BYTES),
        cost_estimate=pl.CostEstimate(flops=flops, bytes_accessed=moved, transcendentals=0),
    )(*args)


def array(*dims):
    return jax.ShapeDtypeStruct(dims, BF16)


def pack(b_ref, out_ref):
    for c in range(2):
        for d in range(GROUP):
            out_ref[d, c, :, 0:PANEL] = b_ref[c, 0]
            parts = [b_ref[c, 1, :, zh * 512 + d * 64 : zh * 512 + d * 64 + 64] for zh in range(ZH)]
            out_ref[d, c, :, PANEL : PANEL + ROWS] = jnp.concatenate(parts, axis=-1)


def complex_parts(prod):
    shots, rows = prod.shape[0] // 2, prod.shape[1] // 2
    real = prod[:shots, :rows] - prod[shots:, rows:]
    imag = prod[:shots, rows:] + prod[shots:, :rows]
    return real, imag


def place_matrix(which, m_ref, mat_ref):
    for src in range(SRC):
        for zh in range(ZH):
            for c in range(2):
                row, col = c * ROWS + zh * 64, src * 128
                mat_ref[row : row + 64, col : col + 128] = m_ref[src, zh, which, c]


def product(v_ref, mat_ref, vec_ref):
    for c in range(2):
        for h in range(ZH):
            for d in range(0, GROUP, 2):
                pair = [v_ref[d + k, c, :, h * 64 : h * 64 + 64] for k in range(2)]
                col = h * 512 + d * 64
                rows = slice(c * GROUP_SHOTS, (c + 1) * GROUP_SHOTS)
                vec_ref[rows, col : col + 128] = jnp.concatenate(pair, axis=-1)
    prod = lax.dot_general(vec_ref[...], mat_ref[...], NT, preferred_element_type=F32)
    return complex_parts(prod)


def first_stage(v_ref, m_ref, rep_ref, first_ref, slice_ref, mat_ref, vec_ref):
    place_matrix(0, m_ref, mat_ref)
    for c in range(2):
        rows = slice(c * GROUP_SHOTS, (c + 1) * GROUP_SHOTS)
        vec_ref[rows, :] = v_ref[:, c, :, 0:PANEL].reshape(GROUP_SHOTS, PANEL)
        slice_ref[c] = v_ref[:, c, :, PANEL : PANEL + ROWS].reshape(GROUP_SHOTS, ROWS)
    prod = lax.dot_general(vec_ref[...], mat_ref[...], NT, preferred_element_type=F32)
    for c, part in enumerate(complex_parts(prod)):
        part = part.astype(BF16)
        first_ref[c] = part
        for d in range(GROUP):
            rep_ref[d, c] = part


def second_stage(v_ref, m_ref, slice_ref, rep_ref, mat_ref, vec_ref):
    place_matrix(1, m_ref, mat_ref)
    for c, part in enumerate(product(v_ref, mat_ref, vec_ref)):
        residual = (slice_ref[c].astype(F32) - part).astype(BF16)
        for d in range(GROUP):
            rep_ref[d, c] = residual


def third_stage(v_ref, m_ref, first_ref, out_ref, mat_ref, vec_ref):
    place_matrix(2, m_ref, mat_ref)
    for c, part in enumerate(product(v_ref, mat_ref, vec_ref)):
        out_ref[:, c, 0] = first_ref[c].reshape(GROUP, SHOTS, ROWS)
        out_ref[:, c, 1] = part.reshape(GROUP, SHOTS, ROWS).astype(BF16)


def unpack(in_ref, out_ref):
    for c in range(2):
        for p in range(2):
            for h in range(ZH):
                for d in range(0, GROUP, 2):
                    pair = [in_ref[d + k, c, p, :, h * 64 : h * 64 + 64] for k in range(2)]
                    col = h * 512 + d * 64
                    out_ref[c, p, :, col : col + 128] = jnp.concatenate(pair, axis=-1)


def exchange(block, axes):
    return lax.all_to_all(block, axes, 0, 0, tiled=True)


def on_device(shot_fields, diag_inverse, coupling):
    group = ("zl", "x")
    block = array(2, GROUP_SHOTS, ROWS)
    repeated = array(GROUP, 2, GROUP_SHOTS, ROWS)

    mats = jnp.stack([diag_inverse[:, 0], coupling, diag_inverse[:, 1]])
    mats = lax.all_gather(mats, "zh", axis=0)
    mats = lax.all_gather(mats, ("y", "core"), axis=0)
    fields = call(pack, array(GROUP, 2, SHOTS, PANEL + ROWS), shot_fields)

    def stage(body, outs, sent, *args):
        scratch = [pltpu.VMEM((2 * ROWS, PANEL), BF16), pltpu.VMEM((2 * GROUP_SHOTS, PANEL), BF16)]
        flops = 2 * 2 * ROWS * PANEL * 2 * GROUP_SHOTS
        fields = exchange(sent, group)
        return call(body, outs, fields, mats, *args, scratch=scratch, flops=flops, moved=3 << 20)

    first_rep, first, second_slice = stage(first_stage, (repeated, block, block), fields)
    residual = stage(second_stage, repeated, first_rep, second_slice)
    both = stage(third_stage, array(GROUP, 2, 2, SHOTS, ROWS), residual, first)
    return call(unpack, array(2, 2, SHOTS, PANEL), exchange(both, group))


def solution(mesh):
    axes = ("zh", "zl", "x", "y", "core")
    fine = Mesh(mesh.devices.reshape(ZH, ZL, X, Y, CORES), axes)
    row, src = axes[:3], axes[3:]
    in_specs = (
        P(None, None, row + src, None),
        P(None, None, row, src),
        P(None, row, src),
    )
    out_specs = P(None, None, row + src, None)
    return jax.shard_map(
        on_device, mesh=fine, in_specs=in_specs, out_specs=out_specs, check_vma=False
    )
```

time: 298 us -> 129 us (0.43)
  waiting for transfers between devices: 200 us -> 32.7 us
  matrix products: 6.78 us -> 0 us
  Pallas kernels: 0 us -> 3.61 us
    all_gather x3 -> x1, waiting for transfers between devices: 200 us -> 32.7 us  [on_device(): mats = lax.all_gather(mats, ('y', 'core'), axis=0)]
    all_to_all x1 -> x4, blocking collectives: 16 us -> 52.3 us  [exchange(): return lax.all_to_all(block, axes, 0, 0, tiled=True)]
    all_gather x3 -> x1, blocking collectives: 55.6 us -> 21 us  [on_device(): mats = lax.all_gather(mats, 'zh', axis=0)]
    dot_general x3 -> x0, matrix products: 6.78 us -> none  [complex_product(): jnp.einsum('csk,drk->cdsr', vector, matrix, preferred_element_type=jnp.fl...]
    pallas_call x0 -> x5, Pallas kernels: none -> 3.61 us  [call(): pl.pallas_call(body, out_shape=outs, in_specs=[VMEM] * len(args), out_spe...]
  transfers between devices with their start and end apart: 3 -> 1, of which waited for: 3 -> 1; matrix products, arithmetic and copies ran while one was open for 0% -> 0% of each run, Pallas kernels for 0% -> 0%
where the time goes in v4:
time: 129 us; the launch traced here: 128 us
  blocking collectives  73.3 us (57%)
  waiting for transfers between devices  32.7 us (25%)
  between operations  13.4 us (10%)
  local copies, waits for them, and re-layouts  4.47 us (3%)
  Pallas kernels  3.61 us (3%)
    all_to_all x4, blocking collectives, exchange(): return lax.all_to_all(block, axes, 0, 0, tiled=True)  52.3 us
    all_gather x1, waiting for transfers between devices, on_device(): mats = lax.all_gather(mats, ('y', 'core'), axis=0)  32.7 us
    all_gather x1, blocking collectives, on_device(): mats = lax.all_gather(mats, 'zh', axis=0)  21 us
    unnamed x6, local copies, waits for them, and re-layouts  3.69 us
    pallas_call x5, Pallas kernels, call(): pl.pallas_call(body, out_shape=outs, in_specs=[VMEM] * len(args), out_spe...  3.61 us
  transfers between devices with their start and end apart: 1, of which 1 were waited for; matrix products, arithmetic and copies ran while one was open for 0% of the time, Pallas kernels for 0%

profile of v4, /device:TPU:8, one launch (start us, length us, event | category | flops | bytes accessed | tf_op | source)
XLA Modules:
  0.0 128.3 jit_solution(4737750722347263823)
XLA Ops:
  6.5 0.0 all-gather.4.cloned.1.call-start
  6.5 0.8 slice_bitcast_fusion.1
  7.3 0.8 pad_maximum_fusion
  8.1 21.0 %all-gather = bf16[12,2,64,128]{3,2,1,0:T(8,128)(2,1)} all-gather(bf16[3,2,64,128]{3,2,1,0:T(8,128)(2,1)S(1)} %pad_maximum_fusion), channel_id=2, replica_groups=mesh['zh'=4,'zl'=2,'x'=4,'y'=8,'core'=2] {'zh'}, dimensions={0}, use_global_device_ids=true | all-gather | bytes 491520 | tf_op jit(solution)/shard_map/all_gather | solution.py:120
  29.1 0.0 all-gather.4.cloned.1.call-update
  29.1 0.0 copy-start.2
  29.1 0.9 copy-done.2
  30.0 0.1 shard_map.37
  30.1 14.7 %all_to_all.20.v_ref = bf16[8,2,8,2304]{3,2,1,0:T(8,128)(2,1)S(1)} all-to-all(bf16[8,2,8,2304]{3,2,1,0:T(8,128)(2,1)S(1)} %shard_map.37), channel_id=1, replica_groups=mesh['zh'=4,'zl'=2,'x'=4,'y'=8,'core'=2] {'zl','x'}, dimensions={0} | all-to-all | bytes 1179648 | tf_op jit(solution)/shard_map/all_to_all | solution.py:111
  44.8 32.7 %all-gather.4.cloned.1.call-done = bf16[64,3,2,64,128]{4,3,2,1,0:T(8,128)(2,1)} async-done(((bf16[4,3,2,64,128]{4,3,2,1,0:T(8,128)(2,1)}), bf16[64,3,2,64,128]{4,3,2,1,0:T(8,128)(2,1)}) %all-gather.4.cloned.1.call-update) | async-done | bytes 6291472 | tf_op jit(solution)/shard_map/all_gather | solution.py:121
  77.5 0.0 copy-start
  77.5 2.8 %copy-done = bf16[64,3,2,64,128]{4,3,2,1,0:T(8,128)(2,1)S(1)} copy-done((bf16[64,3,2,64,128]{4,3,2,1,0:T(8,128)(2,1)S(1)}, bf16[64,3,2,64,128]{4,3,2,1,0:T(8,128)(2,1)}, u32[]{:S(2)}) %copy-start) | copy-done | bytes 6291480
  80.3 0.0 copy-start.1
  80.3 0.9 shard_map.38
  81.2 15.8 %all_to_all.21.v_ref = bf16[8,2,64,256]{3,2,1,0:T(8,128)(2,1)S(1)} all-to-all(bf16[8,2,64,256]{3,2,1,0:T(8,128)(2,1)S(1)} %get-tuple-element.8), channel_id=1, replica_groups=mesh['zh'=4,'zl'=2,'x'=4,'y'=8,'core'=2] {'zl','x'}, dimensions={0} | all-to-all | bytes 1048576 | tf_op jit(solution)/shard_map/all_to_all | solution.py:111
  97.1 0.0 copy-done.1
  97.1 0.9 shard_map.39
  98.0 12.6 %all_to_all.22.v_ref = bf16[8,2,64,256]{3,2,1,0:T(8,128)(2,1)S(1)} all-to-all(bf16[8,2,64,256]{3,2,1,0:T(8,128)(2,1)S(1)} %shard_map.39), channel_id=1, replica_groups=mesh['zh'=4,'zl'=2,'x'=4,'y'=8,'core'=2] {'zl','x'}, dimensions={0} | all-to-all | bytes 1048576 | tf_op jit(solution)/shard_map/all_to_all | solution.py:111
  110.6 0.9 shard_map.40
  111.5 9.1 %all_to_all.23.in_ref = bf16[8,2,2,8,256]{4,3,2,1,0:T(8,128)(2,1)S(1)} all-to-all(bf16[8,2,2,8,256]{4,3,2,1,0:T(8,128)(2,1)S(1)} %shard_map.40), channel_id=1, replica_groups=mesh['zh'=4,'zl'=2,'x'=4,'y'=8,'core'=2] {'zl','x'}, dimensions={0} | all-to-all | bytes 262144 | tf_op jit(solution)/shard_map/all_to_all | solution.py:111
  120.6 0.8 shard_map.41
Async XLA Ops:
  6.5 71.0 %all-gather.4.cloned.1.call-start = ((), (), s32[]{:S(2)}) async-start(), calls=%async_computation.4 | async-start | bytes 6684672 | tf_op jit(solution)/shard_map/all_gather | solution.py:121
  29.1 0.9 copy-start.2
  77.5 2.8 %copy-start = (bf16[64,3,2,64,128]{4,3,2,1,0:T(8,128)(2,1)S(1)}, bf16[64,3,2,64,128]{4,3,2,1,0:T(8,128)(2,1)}, u32[]{:S(2)}) copy-start(bf16[64,3,2,64,128]{4,3,2,1,0:T(8,128)(2,1)} %all-gather.4.cloned.1.call-done) | copy-start | bytes 18874372
  80.3 16.7 %copy-start.1 = (bf16[64,3,2,64,128]{4,3,2,1,0:T(8,128)(2,1)S(1)}, bf16[64,3,2,64,128]{4,3,2,1,0:T(8,128)(2,1)}, u32[]{:S(2)}) copy-start(bf16[64,3,2,64,128]{4,3,2,1,0:T(8,128)(2,1)} %all-gather.4.cloned.1.call-done) | copy-start | bytes 18874372
Sparse Core Ops, SparseCore 0:
  29.2 48.2 all-gather.3

commit v5 on v4

--- a/solution.py
+++ b/solution.py
@@ -14,6 +14,7 @@
 GROUP_SHOTS = GROUP * SHOTS
 VMEM_BYTES = 40 * 1024 * 1024
 VMEM = pl.BlockSpec(memory_space=pltpu.VMEM)
+FIRST, SECOND, COUPLING = (0, 2), (1, 3), (4, 5)
 NT = (((1,), (1,)), ((), ()))
 
 
@@ -48,12 +49,12 @@
     return real, imag
 
 
-def place_matrix(which, m_ref, mat_ref):
+def place_matrix(pair, m_ref, mat_ref):
     for src in range(SRC):
         for zh in range(ZH):
             for c in range(2):
                 row, col = c * ROWS + zh * 64, src * 128
-                mat_ref[row : row + 64, col : col + 128] = m_ref[src, zh, which, c]
+                mat_ref[row : row + 64, col : col + 128] = m_ref[src, zh, pair[c]]
 
 
 def product(v_ref, mat_ref, vec_ref):
@@ -69,7 +70,7 @@
 
 
 def first_stage(v_ref, m_ref, rep_ref, first_ref, slice_ref, mat_ref, vec_ref):
-    place_matrix(0, m_ref, mat_ref)
+    place_matrix(FIRST, m_ref, mat_ref)
     for c in range(2):
         rows = slice(c * GROUP_SHOTS, (c + 1) * GROUP_SHOTS)
         vec_ref[rows, :] = v_ref[:, c, :, 0:PANEL].reshape(GROUP_SHOTS, PANEL)
@@ -83,7 +84,7 @@
 
 
 def second_stage(v_ref, m_ref, slice_ref, rep_ref, mat_ref, vec_ref):
-    place_matrix(1, m_ref, mat_ref)
+    place_matrix(COUPLING, m_ref, mat_ref)
     for c, part in enumerate(product(v_ref, mat_ref, vec_ref)):
         residual = (slice_ref[c].astype(F32) - part).astype(BF16)
         for d in range(GROUP):
@@ -91,7 +92,7 @@
 
 
 def third_stage(v_ref, m_ref, first_ref, out_ref, mat_ref, vec_ref):
-    place_matrix(2, m_ref, mat_ref)
+    place_matrix(SECOND, m_ref, mat_ref)
     for c, part in enumerate(product(v_ref, mat_ref, vec_ref)):
         out_ref[:, c, 0] = first_ref[c].reshape(GROUP, SHOTS, ROWS)
         out_ref[:, c, 1] = part.reshape(GROUP, SHOTS, ROWS).astype(BF16)
@@ -116,7 +117,7 @@
     block = array(2, GROUP_SHOTS, ROWS)
     repeated = array(GROUP, 2, GROUP_SHOTS, ROWS)
 
-    mats = jnp.stack([diag_inverse[:, 0], coupling, diag_inverse[:, 1]])
+    mats = jnp.concatenate([diag_inverse.reshape(4, 64, 128), coupling])
     mats = lax.all_gather(mats, "zh", axis=0)
     mats = lax.all_gather(mats, ("y", "core"), axis=0)
     fields = call(pack, array(GROUP, 2, SHOTS, PANEL + ROWS), shot_fields)

time: 129 us -> 128 us (level)
  no operation moved by 1% of the time
where the time goes in v5:
time: 128 us
  blocking collectives  73.3 us (57%)
  waiting for transfers between devices  32.7 us (26%)
  between operations  13.4 us (10%)
  local copies, waits for them, and re-layouts  3.69 us (3%)
  Pallas kernels  3.6 us (3%)
    all_to_all x4, blocking collectives, exchange(): return lax.all_to_all(block, axes, 0, 0, tiled=True)  52.3 us
    all_gather x1, waiting for transfers between devices, on_device(): mats = lax.all_gather(mats, ('y', 'core'), axis=0)  32.7 us
    all_gather x1, blocking collectives, on_device(): mats = lax.all_gather(mats, 'zh', axis=0)  21 us
    unnamed x6, local copies, waits for them, and re-layouts  3.69 us
    pallas_call x5, Pallas kernels, call(): pl.pallas_call(body, out_shape=outs, in_specs=[VMEM] * len(args), out_spe...  3.6 us
  transfers between devices with their start and end apart: 1, of which 1 were waited for; matrix products, arithmetic and copies ran while one was open for 0% of the time, Pallas kernels for 0%

profile of v5, /device:TPU:8, one launch (start us, length us, event | category | flops | bytes accessed | tf_op | source)
XLA Modules:
  0.0 127.6 jit_solution(3577227363061411960)
XLA Ops:
  6.5 0.0 all-gather.4.cloned.1.call-start
  6.5 0.9 pad_maximum_fusion
  7.4 21.0 %all-gather = bf16[24,64,128]{2,1,0:T(8,128)(2,1)} all-gather(bf16[6,64,128]{2,1,0:T(8,128)(2,1)S(1)} %pad_maximum_fusion), channel_id=2, replica_groups=mesh['zh'=4,'zl'=2,'x'=4,'y'=8,'core'=2] {'zh'}, dimensions={0}, use_global_device_ids=true | all-gather | bytes 491520 | tf_op jit(solution)/shard_map/all_gather | solution.py:121
  28.4 0.0 all-gather.4.cloned.1.call-update
  28.4 0.0 copy-start.2
  28.4 0.9 copy-done.2
  29.3 0.1 shard_map.37
  29.4 14.7 %all_to_all.20.v_ref = bf16[8,2,8,2304]{3,2,1,0:T(8,128)(2,1)S(1)} all-to-all(bf16[8,2,8,2304]{3,2,1,0:T(8,128)(2,1)S(1)} %shard_map.37), channel_id=1, replica_groups=mesh['zh'=4,'zl'=2,'x'=4,'y'=8,'core'=2] {'zl','x'}, dimensions={0} | all-to-all | bytes 1179648 | tf_op jit(solution)/shard_map/all_to_all | solution.py:112
  44.2 32.7 %all-gather.4.cloned.1.call-done = bf16[64,6,64,128]{3,2,1,0:T(8,128)(2,1)} async-done(((bf16[4,6,64,128]{3,2,1,0:T(8,128)(2,1)}), bf16[64,6,64,128]{3,2,1,0:T(8,128)(2,1)}) %all-gather.4.cloned.1.call-update) | async-done | bytes 6291472 | tf_op jit(solution)/shard_map/all_gather | solution.py:122
  76.9 0.0 copy-start
  76.9 2.8 %copy-done = bf16[64,6,64,128]{3,2,1,0:T(8,128)(2,1)S(1)} copy-done((bf16[64,6,64,128]{3,2,1,0:T(8,128)(2,1)S(1)}, bf16[64,6,64,128]{3,2,1,0:T(8,128)(2,1)}, u32[]{:S(2)}) %copy-start) | copy-done | bytes 6291480
  79.6 0.0 copy-start.1
  79.6 0.9 shard_map.38
  80.6 15.8 %all_to_all.21.v_ref = bf16[8,2,64,256]{3,2,1,0:T(8,128)(2,1)S(1)} all-to-all(bf16[8,2,64,256]{3,2,1,0:T(8,128)(2,1)S(1)} %get-tuple-element.8), channel_id=1, replica_groups=mesh['zh'=4,'zl'=2,'x'=4,'y'=8,'core'=2] {'zl','x'}, dimensions={0} | all-to-all | bytes 1048576 | tf_op jit(solution)/shard_map/all_to_all | solution.py:112
  96.4 0.0 copy-done.1
  96.4 0.9 shard_map.39
  97.3 12.6 %all_to_all.22.v_ref = bf16[8,2,64,256]{3,2,1,0:T(8,128)(2,1)S(1)} all-to-all(bf16[8,2,64,256]{3,2,1,0:T(8,128)(2,1)S(1)} %shard_map.39), channel_id=1, replica_groups=mesh['zh'=4,'zl'=2,'x'=4,'y'=8,'core'=2] {'zl','x'}, dimensions={0} | all-to-all | bytes 1048576 | tf_op jit(solution)/shard_map/all_to_all | solution.py:112
  109.9 0.9 shard_map.40
  110.8 9.1 %all_to_all.23.in_ref = bf16[8,2,2,8,256]{4,3,2,1,0:T(8,128)(2,1)S(1)} all-to-all(bf16[8,2,2,8,256]{4,3,2,1,0:T(8,128)(2,1)S(1)} %shard_map.40), channel_id=1, replica_groups=mesh['zh'=4,'zl'=2,'x'=4,'y'=8,'core'=2] {'zl','x'}, dimensions={0} | all-to-all | bytes 262144 | tf_op jit(solution)/shard_map/all_to_all | solution.py:112
  120.0 0.8 shard_map.41
Async XLA Ops:
  6.5 70.3 %all-gather.4.cloned.1.call-start = ((), (), s32[]{:S(2)}) async-start(), calls=%async_computation.4 | async-start | bytes 6684672 | tf_op jit(solution)/shard_map/all_gather | solution.py:122
  28.4 0.9 copy-start.2
  76.9 2.8 %copy-start = (bf16[64,6,64,128]{3,2,1,0:T(8,128)(2,1)S(1)}, bf16[64,6,64,128]{3,2,1,0:T(8,128)(2,1)}, u32[]{:S(2)}) copy-start(bf16[64,6,64,128]{3,2,1,0:T(8,128)(2,1)} %all-gather.4.cloned.1.call-done) | copy-start | bytes 18874372
  79.6 16.7 %copy-start.1 = (bf16[64,6,64,128]{3,2,1,0:T(8,128)(2,1)S(1)}, bf16[64,6,64,128]{3,2,1,0:T(8,128)(2,1)}, u32[]{:S(2)}) copy-start(bf16[64,6,64,128]{3,2,1,0:T(8,128)(2,1)} %all-gather.4.cloned.1.call-done) | copy-start | bytes 18874372
Sparse Core Ops, SparseCore 0:
  28.5 48.2 all-gather.3

commit v6 on v5

--- a/solution.py
+++ b/solution.py
@@ -69,12 +69,15 @@
     return complex_parts(prod)
 
 
-def first_stage(v_ref, m_ref, rep_ref, first_ref, slice_ref, mat_ref, vec_ref):
-    place_matrix(FIRST, m_ref, mat_ref)
+def place_fields(v_ref, vec_ref, slice_ref):
     for c in range(2):
         rows = slice(c * GROUP_SHOTS, (c + 1) * GROUP_SHOTS)
         vec_ref[rows, :] = v_ref[:, c, :, 0:PANEL].reshape(GROUP_SHOTS, PANEL)
         slice_ref[c] = v_ref[:, c, :, PANEL : PANEL + ROWS].reshape(GROUP_SHOTS, ROWS)
+
+
+def first_stage(vec_ref, m_ref, rep_ref, first_ref, mat_ref):
+    place_matrix(FIRST, m_ref, mat_ref)
     prod = lax.dot_general(vec_ref[...], mat_ref[...], NT, preferred_element_type=F32)
     for c, part in enumerate(complex_parts(prod)):
         part = part.astype(BF16)
@@ -122,13 +125,26 @@
     mats = lax.all_gather(mats, ("y", "core"), axis=0)
     fields = call(pack, array(GROUP, 2, SHOTS, PANEL + ROWS), shot_fields)
 
+    flops = 2 * 2 * ROWS * PANEL * 2 * GROUP_SHOTS
+    matrix, vector = pltpu.VMEM((2 * ROWS, PANEL), BF16), pltpu.VMEM((2 * GROUP_SHOTS, PANEL), BF16)
+
     def stage(body, outs, sent, *args):
-        scratch = [pltpu.VMEM((2 * ROWS, PANEL), BF16), pltpu.VMEM((2 * GROUP_SHOTS, PANEL), BF16)]
-        flops = 2 * 2 * ROWS * PANEL * 2 * GROUP_SHOTS
         fields = exchange(sent, group)
+        scratch = [matrix, vector]
         return call(body, outs, fields, mats, *args, scratch=scratch, flops=flops, moved=3 << 20)
 
-    first_rep, first, second_slice = stage(first_stage, (repeated, block, block), fields)
+    placed, second_slice = call(
+        place_fields, (array(2 * GROUP_SHOTS, PANEL), block), exchange(fields, group)
+    )
+    first_rep, first = call(
+        first_stage,
+        (repeated, block),
+        placed,
+        mats,
+        scratch=[matrix],
+        flops=flops,
+        moved=3 << 20,
+    )
     residual = stage(second_stage, repeated, first_rep, second_slice)
     both = stage(third_stage, array(GROUP, 2, 2, SHOTS, ROWS), residual, first)
     return call(unpack, array(2, 2, SHOTS, PANEL), exchange(both, group))

time: 128 us -> 128 us (level)
    pallas_call x5 -> x6, Pallas kernels: 3.6 us -> 3.64 us  [call(): pl.pallas_call(body, out_shape=outs, in_specs=[VMEM] * len(args), out_spe...]
where the time goes in v6:
time: 128 us
  blocking collectives  73.3 us (57%)
  waiting for transfers between devices  32.7 us (26%)
  between operations  13.4 us (10%)
  local copies, waits for them, and re-layouts  3.69 us (3%)
  Pallas kernels  3.64 us (3%)
    all_to_all x4, blocking collectives, exchange(): return lax.all_to_all(block, axes, 0, 0, tiled=True)  52.3 us
    all_gather x1, waiting for transfers between devices, on_device(): mats = lax.all_gather(mats, ('y', 'core'), axis=0)  32.7 us
    all_gather x1, blocking collectives, on_device(): mats = lax.all_gather(mats, 'zh', axis=0)  21 us
    unnamed x6, local copies, waits for them, and re-layouts  3.69 us
    pallas_call x6, Pallas kernels, call(): pl.pallas_call(body, out_shape=outs, in_specs=[VMEM] * len(args), out_spe...  3.64 us
  transfers between devices with their start and end apart: 1, of which 1 were waited for; matrix products, arithmetic and copies ran while one was open for 0% of the time, Pallas kernels for 0%

profile of v6, /device:TPU:8, one launch (start us, length us, event | category | flops | bytes accessed | tf_op | source)
XLA Modules:
  0.0 127.6 jit_solution(15028299098671526211)
XLA Ops:
  6.5 0.0 all-gather.4.cloned.1.call-start
  6.5 0.9 pad_maximum_fusion
  7.4 21.0 %all-gather = bf16[24,64,128]{2,1,0:T(8,128)(2,1)} all-gather(bf16[6,64,128]{2,1,0:T(8,128)(2,1)S(1)} %pad_maximum_fusion), channel_id=2, replica_groups=mesh['zh'=4,'zl'=2,'x'=4,'y'=8,'core'=2] {'zh'}, dimensions={0}, use_global_device_ids=true | all-gather | bytes 491520 | tf_op jit(solution)/shard_map/all_gather | solution.py:124
  28.4 0.0 all-gather.4.cloned.1.call-update
  28.4 0.0 copy-start.2
  28.4 0.9 copy-done.2
  29.3 0.1 shard_map.37
  29.4 14.7 %all_to_all.20.v_ref = bf16[8,2,8,2304]{3,2,1,0:T(8,128)(2,1)S(1)} all-to-all(bf16[8,2,8,2304]{3,2,1,0:T(8,128)(2,1)S(1)} %shard_map.37), channel_id=1, replica_groups=mesh['zh'=4,'zl'=2,'x'=4,'y'=8,'core'=2] {'zl','x'}, dimensions={0} | all-to-all | bytes 1179648 | tf_op jit(solution)/shard_map/all_to_all | solution.py:115
  44.2 32.7 %all-gather.4.cloned.1.call-done = bf16[64,6,64,128]{3,2,1,0:T(8,128)(2,1)} async-done(((bf16[4,6,64,128]{3,2,1,0:T(8,128)(2,1)}), bf16[64,6,64,128]{3,2,1,0:T(8,128)(2,1)}) %all-gather.4.cloned.1.call-update) | async-done | bytes 6291472 | tf_op jit(solution)/shard_map/all_gather | solution.py:125
  76.9 0.0 copy-start
  76.9 2.8 %copy-done = bf16[64,6,64,128]{3,2,1,0:T(8,128)(2,1)S(1)} copy-done((bf16[64,6,64,128]{3,2,1,0:T(8,128)(2,1)S(1)}, bf16[64,6,64,128]{3,2,1,0:T(8,128)(2,1)}, u32[]{:S(2)}) %copy-start) | copy-done | bytes 6291480
  79.6 0.0 copy-start.1
  79.6 0.9 shard_map.39
  80.6 15.8 %all_to_all.21.v_ref = bf16[8,2,64,256]{3,2,1,0:T(8,128)(2,1)S(1)} all-to-all(bf16[8,2,64,256]{3,2,1,0:T(8,128)(2,1)S(1)} %get-tuple-element.10), channel_id=1, replica_groups=mesh['zh'=4,'zl'=2,'x'=4,'y'=8,'core'=2] {'zl','x'}, dimensions={0} | all-to-all | bytes 1048576 | tf_op jit(solution)/shard_map/all_to_all | solution.py:115
  96.4 0.0 copy-done.1
  96.4 0.9 shard_map.40
  97.3 12.6 %all_to_all.22.v_ref = bf16[8,2,64,256]{3,2,1,0:T(8,128)(2,1)S(1)} all-to-all(bf16[8,2,64,256]{3,2,1,0:T(8,128)(2,1)S(1)} %shard_map.40), channel_id=1, replica_groups=mesh['zh'=4,'zl'=2,'x'=4,'y'=8,'core'=2] {'zl','x'}, dimensions={0} | all-to-all | bytes 1048576 | tf_op jit(solution)/shard_map/all_to_all | solution.py:115
  109.9 0.9 shard_map.41
  110.8 9.1 %all_to_all.23.in_ref = bf16[8,2,2,8,256]{4,3,2,1,0:T(8,128)(2,1)S(1)} all-to-all(bf16[8,2,2,8,256]{4,3,2,1,0:T(8,128)(2,1)S(1)} %shard_map.41), channel_id=1, replica_groups=mesh['zh'=4,'zl'=2,'x'=4,'y'=8,'core'=2] {'zl','x'}, dimensions={0} | all-to-all | bytes 262144 | tf_op jit(solution)/shard_map/all_to_all | solution.py:115
  120.0 0.8 shard_map.42
  (1 shorter events, 0.0 us)
Async XLA Ops:
  6.5 70.3 %all-gather.4.cloned.1.call-start = ((), (), s32[]{:S(2)}) async-start(), calls=%async_computation.4 | async-start | bytes 6684672 | tf_op jit(solution)/shard_map/all_gather | solution.py:125
  28.4 0.9 copy-start.2
  76.9 2.8 %copy-start = (bf16[64,6,64,128]{3,2,1,0:T(8,128)(2,1)S(1)}, bf16[64,6,64,128]{3,2,1,0:T(8,128)(2,1)}, u32[]{:S(2)}) copy-start(bf16[64,6,64,128]{3,2,1,0:T(8,128)(2,1)} %all-gather.4.cloned.1.call-done) | copy-start | bytes 18874372
  79.6 16.7 %copy-start.1 = (bf16[64,6,64,128]{3,2,1,0:T(8,128)(2,1)S(1)}, bf16[64,6,64,128]{3,2,1,0:T(8,128)(2,1)}, u32[]{:S(2)}) copy-start(bf16[64,6,64,128]{3,2,1,0:T(8,128)(2,1)} %all-gather.4.cloned.1.call-done) | copy-start | bytes 18874372
Sparse Core Ops, SparseCore 0:
  28.5 48.2 all-gather.3

commit v7 on v5

--- a/solution.py
+++ b/solution.py
@@ -118,7 +118,7 @@
     repeated = array(GROUP, 2, GROUP_SHOTS, ROWS)
 
     mats = jnp.concatenate([diag_inverse.reshape(4, 64, 128), coupling])
-    mats = lax.all_gather(mats, "zh", axis=0)
+    mats = exchange(jnp.broadcast_to(mats[None], (ZH,) + mats.shape), "zh")
     mats = lax.all_gather(mats, ("y", "core"), axis=0)
     fields = call(pack, array(GROUP, 2, SHOTS, PANEL + ROWS), shot_fields)
 

time: 128 us -> 128 us (level)
  blocking collectives: 73.3 us -> 76.5 us
  waiting for transfers between devices: 32.7 us -> 29.5 us
    all_to_all x4 -> x5, blocking collectives: 52.3 us -> 76.5 us  [exchange(): return lax.all_to_all(block, axes, 0, 0, tiled=True)]
    all_gather x1 -> x0, blocking collectives: 21 us -> none  [on_device(): mats = lax.all_gather(mats, 'zh', axis=0)]
    all_gather x1, waiting for transfers between devices: 32.7 us -> 29.5 us  [on_device(): mats = lax.all_gather(mats, ('y', 'core'), axis=0)]
where the time goes in v7:
time: 128 us
  blocking collectives  76.5 us (60%)
  waiting for transfers between devices  29.5 us (23%)
  between operations  13.4 us (10%)
  local copies, waits for them, and re-layouts  3.76 us (3%)
  Pallas kernels  3.6 us (3%)
    all_to_all x5, blocking collectives, exchange(): return lax.all_to_all(block, axes, 0, 0, tiled=True)  76.5 us
    all_gather x1, waiting for transfers between devices, on_device(): mats = lax.all_gather(mats, ('y', 'core'), axis=0)  29.5 us
    unnamed x6, local copies, waits for them, and re-layouts  3.69 us
    pallas_call x5, Pallas kernels, call(): pl.pallas_call(body, out_shape=outs, in_specs=[VMEM] * len(args), out_spe...  3.6 us
  transfers between devices with their start and end apart: 1, of which 1 were waited for; matrix products, arithmetic and copies ran while one was open for 0% of the time, Pallas kernels for 0%

profile of v7, /device:TPU:8, one launch (start us, length us, event | category | flops | bytes accessed | tf_op | source)
XLA Modules:
  0.0 127.7 jit_solution(3624628070674280176)
XLA Ops:
  6.5 0.0 all-gather.3.cloned.1.call-start
  6.5 0.9 pad_maximum_fusion
  7.4 0.1 broadcast_in_dim.2
  7.5 24.5 %all_to_all.25 = bf16[4,6,64,128]{3,2,1,0:T(8,128)(2,1)} all-to-all(bf16[4,6,64,128]{3,2,1,0:T(8,128)(2,1)S(1)} %broadcast_in_dim.2), channel_id=1, replica_groups=mesh['zh'=4,'zl'=2,'x'=4,'y'=8,'core'=2] {'zh'}, dimensions={0} | all-to-all | bytes 786432 | tf_op jit(solution)/shard_map/all_to_all | solution.py:112
  32.0 0.0 all-gather.3.cloned.1.call-update
  32.0 0.0 copy-start.2
  32.1 0.9 copy-done.2
  32.9 0.1 shard_map.37
  33.1 14.4 %all_to_all.26.v_ref = bf16[8,2,8,2304]{3,2,1,0:T(8,128)(2,1)S(1)} all-to-all(bf16[8,2,8,2304]{3,2,1,0:T(8,128)(2,1)S(1)} %shard_map.37), channel_id=1, replica_groups=mesh['zh'=4,'zl'=2,'x'=4,'y'=8,'core'=2] {'zl','x'}, dimensions={0} | all-to-all | bytes 1179648 | tf_op jit(solution)/shard_map/all_to_all | solution.py:112
  47.5 29.5 %all-gather.3.cloned.1.call-done = bf16[64,6,64,128]{3,2,1,0:T(8,128)(2,1)} async-done(((bf16[4,6,64,128]{3,2,1,0:T(8,128)(2,1)}), bf16[64,6,64,128]{3,2,1,0:T(8,128)(2,1)}) %all-gather.3.cloned.1.call-update) | async-done | bytes 6291472 | tf_op jit(solution)/shard_map/all_gather | solution.py:122
  76.9 0.0 copy-start
  76.9 2.8 %copy-done = bf16[64,6,64,128]{3,2,1,0:T(8,128)(2,1)S(1)} copy-done((bf16[64,6,64,128]{3,2,1,0:T(8,128)(2,1)S(1)}, bf16[64,6,64,128]{3,2,1,0:T(8,128)(2,1)}, u32[]{:S(2)}) %copy-start) | copy-done | bytes 6291480
  79.7 0.0 copy-start.1
  79.7 0.9 shard_map.38
  80.6 15.8 %all_to_all.27.v_ref = bf16[8,2,64,256]{3,2,1,0:T(8,128)(2,1)S(1)} all-to-all(bf16[8,2,64,256]{3,2,1,0:T(8,128)(2,1)S(1)} %get-tuple-element.8), channel_id=1, replica_groups=mesh['zh'=4,'zl'=2,'x'=4,'y'=8,'core'=2] {'zl','x'}, dimensions={0} | all-to-all | bytes 1048576 | tf_op jit(solution)/shard_map/all_to_all | solution.py:112
  96.5 0.0 copy-done.1
  96.5 0.9 shard_map.39
  97.4 12.6 %all_to_all.28.v_ref = bf16[8,2,64,256]{3,2,1,0:T(8,128)(2,1)S(1)} all-to-all(bf16[8,2,64,256]{3,2,1,0:T(8,128)(2,1)S(1)} %shard_map.39), channel_id=1, replica_groups=mesh['zh'=4,'zl'=2,'x'=4,'y'=8,'core'=2] {'zl','x'}, dimensions={0} | all-to-all | bytes 1048576 | tf_op jit(solution)/shard_map/all_to_all | solution.py:112
  110.0 0.9 shard_map.40
  110.9 9.1 %all_to_all.29.in_ref = bf16[8,2,2,8,256]{4,3,2,1,0:T(8,128)(2,1)S(1)} all-to-all(bf16[8,2,2,8,256]{4,3,2,1,0:T(8,128)(2,1)S(1)} %shard_map.40), channel_id=1, replica_groups=mesh['zh'=4,'zl'=2,'x'=4,'y'=8,'core'=2] {'zl','x'}, dimensions={0} | all-to-all | bytes 262144 | tf_op jit(solution)/shard_map/all_to_all | solution.py:112
  120.0 0.8 shard_map.41
Async XLA Ops:
  6.5 70.4 %all-gather.3.cloned.1.call-start = ((), (), s32[]{:S(2)}) async-start(), calls=%async_computation.5 | async-start | bytes 6684672 | tf_op jit(solution)/shard_map/all_gather | solution.py:122
  32.0 0.9 copy-start.2
  76.9 2.8 %copy-start = (bf16[64,6,64,128]{3,2,1,0:T(8,128)(2,1)S(1)}, bf16[64,6,64,128]{3,2,1,0:T(8,128)(2,1)}, u32[]{:S(2)}) copy-start(bf16[64,6,64,128]{3,2,1,0:T(8,128)(2,1)} %all-gather.3.cloned.1.call-done) | copy-start | bytes 18874372
  79.7 16.8 %copy-start.1 = (bf16[64,6,64,128]{3,2,1,0:T(8,128)(2,1)S(1)}, bf16[64,6,64,128]{3,2,1,0:T(8,128)(2,1)}, u32[]{:S(2)}) copy-start(bf16[64,6,64,128]{3,2,1,0:T(8,128)(2,1)} %all-gather.3.cloned.1.call-done) | copy-start | bytes 18874372
Sparse Core Ops, SparseCore 0:
  32.2 44.7 all-gather.2

commit v8 on v5

--- a/solution.py
+++ b/solution.py
@@ -12,7 +12,7 @@
 PANEL, SHOTS = 2048, 8
 ROWS = PANEL // GROUP
 GROUP_SHOTS = GROUP * SHOTS
-VMEM_BYTES = 40 * 1024 * 1024
+VMEM_BYTES = 16 * 1024 * 1024
 VMEM = pl.BlockSpec(memory_space=pltpu.VMEM)
 FIRST, SECOND, COUPLING = (0, 2), (1, 3), (4, 5)
 NT = (((1,), (1,)), ((), ()))

time: 128 us -> 128 us (level)
  no operation moved by 1% of the time
where the time goes in v8:
time: 128 us
  blocking collectives  73.3 us (57%)
  waiting for transfers between devices  32.7 us (26%)
  between operations  13.4 us (10%)
  local copies, waits for them, and re-layouts  3.69 us (3%)
  Pallas kernels  3.6 us (3%)
    all_to_all x4, blocking collectives, exchange(): return lax.all_to_all(block, axes, 0, 0, tiled=True)  52.3 us
    all_gather x1, waiting for transfers between devices, on_device(): mats = lax.all_gather(mats, ('y', 'core'), axis=0)  32.7 us
    all_gather x1, blocking collectives, on_device(): mats = lax.all_gather(mats, 'zh', axis=0)  21 us
    unnamed x6, local copies, waits for them, and re-layouts  3.69 us
    pallas_call x5, Pallas kernels, call(): pl.pallas_call(body, out_shape=outs, in_specs=[VMEM] * len(args), out_spe...  3.6 us
  transfers between devices with their start and end apart: 1, of which 1 were waited for; matrix products, arithmetic and copies ran while one was open for 0% of the time, Pallas kernels for 0%

profile of v8, /device:TPU:8, one launch (start us, length us, event | category | flops | bytes accessed | tf_op | source)
XLA Modules:
  0.0 127.6 jit_solution(5617022400591516432)
XLA Ops:
  6.5 0.0 all-gather.4.cloned.1.call-start
  6.5 0.9 pad_maximum_fusion
  7.4 21.0 %all-gather = bf16[24,64,128]{2,1,0:T(8,128)(2,1)} all-gather(bf16[6,64,128]{2,1,0:T(8,128)(2,1)S(1)} %pad_maximum_fusion), channel_id=2, replica_groups=mesh['zh'=4,'zl'=2,'x'=4,'y'=8,'core'=2] {'zh'}, dimensions={0}, use_global_device_ids=true | all-gather | bytes 491520 | tf_op jit(solution)/shard_map/all_gather | solution.py:121
  28.4 0.0 all-gather.4.cloned.1.call-update
  28.4 0.0 copy-start.2
  28.4 0.9 copy-done.2
  29.3 0.1 shard_map.37
  29.4 14.7 %all_to_all.20.v_ref = bf16[8,2,8,2304]{3,2,1,0:T(8,128)(2,1)S(1)} all-to-all(bf16[8,2,8,2304]{3,2,1,0:T(8,128)(2,1)S(1)} %shard_map.37), channel_id=1, replica_groups=mesh['zh'=4,'zl'=2,'x'=4,'y'=8,'core'=2] {'zl','x'}, dimensions={0} | all-to-all | bytes 1179648 | tf_op jit(solution)/shard_map/all_to_all | solution.py:112
  44.2 32.7 %all-gather.4.cloned.1.call-done = bf16[64,6,64,128]{3,2,1,0:T(8,128)(2,1)} async-done(((bf16[4,6,64,128]{3,2,1,0:T(8,128)(2,1)}), bf16[64,6,64,128]{3,2,1,0:T(8,128)(2,1)}) %all-gather.4.cloned.1.call-update) | async-done | bytes 6291472 | tf_op jit(solution)/shard_map/all_gather | solution.py:122
  76.9 0.0 copy-start
  76.9 2.8 %copy-done = bf16[64,6,64,128]{3,2,1,0:T(8,128)(2,1)S(1)} copy-done((bf16[64,6,64,128]{3,2,1,0:T(8,128)(2,1)S(1)}, bf16[64,6,64,128]{3,2,1,0:T(8,128)(2,1)}, u32[]{:S(2)}) %copy-start) | copy-done | bytes 6291480
  79.6 0.0 copy-start.1
  79.6 0.9 shard_map.38
  80.6 15.8 %all_to_all.21.v_ref = bf16[8,2,64,256]{3,2,1,0:T(8,128)(2,1)S(1)} all-to-all(bf16[8,2,64,256]{3,2,1,0:T(8,128)(2,1)S(1)} %get-tuple-element.8), channel_id=1, replica_groups=mesh['zh'=4,'zl'=2,'x'=4,'y'=8,'core'=2] {'zl','x'}, dimensions={0} | all-to-all | bytes 1048576 | tf_op jit(solution)/shard_map/all_to_all | solution.py:112
  96.4 0.0 copy-done.1
  96.4 0.9 shard_map.39
  97.3 12.6 %all_to_all.22.v_ref = bf16[8,2,64,256]{3,2,1,0:T(8,128)(2,1)S(1)} all-to-all(bf16[8,2,64,256]{3,2,1,0:T(8,128)(2,1)S(1)} %shard_map.39), channel_id=1, replica_groups=mesh['zh'=4,'zl'=2,'x'=4,'y'=8,'core'=2] {'zl','x'}, dimensions={0} | all-to-all | bytes 1048576 | tf_op jit(solution)/shard_map/all_to_all | solution.py:112
  109.9 0.9 shard_map.40
  110.8 9.1 %all_to_all.23.in_ref = bf16[8,2,2,8,256]{4,3,2,1,0:T(8,128)(2,1)S(1)} all-to-all(bf16[8,2,2,8,256]{4,3,2,1,0:T(8,128)(2,1)S(1)} %shard_map.40), channel_id=1, replica_groups=mesh['zh'=4,'zl'=2,'x'=4,'y'=8,'core'=2] {'zl','x'}, dimensions={0} | all-to-all | bytes 262144 | tf_op jit(solution)/shard_map/all_to_all | solution.py:112
  120.0 0.8 shard_map.41
Async XLA Ops:
  6.5 70.3 %all-gather.4.cloned.1.call-start = ((), (), s32[]{:S(2)}) async-start(), calls=%async_computation.4 | async-start | bytes 6684672 | tf_op jit(solution)/shard_map/all_gather | solution.py:122
  28.4 0.9 copy-start.2
  76.9 2.8 %copy-start = (bf16[64,6,64,128]{3,2,1,0:T(8,128)(2,1)S(1)}, bf16[64,6,64,128]{3,2,1,0:T(8,128)(2,1)}, u32[]{:S(2)}) copy-start(bf16[64,6,64,128]{3,2,1,0:T(8,128)(2,1)} %all-gather.4.cloned.1.call-done) | copy-start | bytes 18874372
  79.6 16.7 %copy-start.1 = (bf16[64,6,64,128]{3,2,1,0:T(8,128)(2,1)S(1)}, bf16[64,6,64,128]{3,2,1,0:T(8,128)(2,1)}, u32[]{:S(2)}) copy-start(bf16[64,6,64,128]{3,2,1,0:T(8,128)(2,1)} %all-gather.4.cloned.1.call-done) | copy-start | bytes 18874372
Sparse Core Ops, SparseCore 0:
  28.5 48.2 all-gather.3
